TPU v7x, 32 devices: a whole 2x2x4 slice. The times are simulated.
32 devices in a mesh: dx: 4 (over z), dy: 8 (over y, x, core).
Axes of the slice: x: 2, y: 2, z: 4, core: 2. Of those that a mesh axis runs over, the one named last changes fastest.
Arguments:
- orbitals: bfloat16 [32, 64, 4096], P(('dx', 'dy')), may hold values from -6 to 6
- offsets: int32 [32, 3], replicated, may hold values from 0 to 31
- pair_list: int32 [256, 2], P(('dx', 'dy')), may hold values from 0 to 31, as said below
- pair_mask: int32 [256], P(('dx', 'dy')), may hold values from 0 to 1, as said below
Outputs:
- exchange: float32 [32, 64, 4096], P(('dx', 'dy'))
Inputs may be any that keep to these rules, and one draw needn't show every extreme that they name: `pair_list`: in each spatial domain's block of 8 slots (domain index dx * 8 + dy owns orbitals 1 * that index onward), the first orbital belongs to that domain and the second to it or to one of the eight domains whose x and y domain indices differ by at most one, wrapping around. `pair_mask`: every domain uses at least one slot; in every draw some domain uses all 8.
All inputs are finite; a program needn't handle non-finite values.
Results may differ from a plain program's by a relative error of at most 0.0003.
Values may be sent and summed in bfloat16 or wider, within the bound.
A program may use at most 64 MiB of HBM per device.

v0:
```python
import math

import jax
import jax.numpy as jnp
from jax import lax
from jax.sharding import PartitionSpec as P


def extended(value, sides, width):
    for axis, dim in sides:
        size, length = (lax.axis_size(axis), value.shape[dim])
        up = [(i, (i + 1) % size) for i in range(size)]
        down = [(j, i) for i, j in up]
        last = lax.slice_in_dim(value, length - width, length, axis=dim)
        leading = lax.slice_in_dim(value, 0, width, axis=dim)
        before = lax.ppermute(last, axis, up)
        after = lax.ppermute(leading, axis, down)
        value = jnp.concatenate([before, value, after], axis=dim)
    return value


def shifted(value, axis, steps):
    count = lax.axis_size(axis)
    pairs = [(source, (source + steps) % count) for source in range(count)]
    return lax.ppermute(value, axis, pairs)


def shift_box(field, sx, sy, sz):
    box = field.shape[0]
    flat = field.shape[1]
    padded = jnp.pad(field, ((box, box), (0, 0)))
    field = lax.dynamic_slice_in_dim(padded, box + sx, box, 0)
    padded = jnp.pad(field, ((0, 0), (flat, flat)))
    field = lax.dynamic_slice_in_dim(padded, flat + sy * box, flat, 1)
    padded = jnp.pad(field, ((0, 0), (box, box)))
    field = lax.dynamic_slice_in_dim(padded, box + sz, flat, 1)
    column = jnp.arange(flat, dtype=jnp.int32) % box + sz
    keep = (column >= 0) & (column < box)
    return jnp.where(keep[None, :], field, jnp.zeros_like(field))


def kernel_tiled(box):
    freq = jnp.arange(box, dtype=jnp.int32)
    freq = freq - box * (freq >= box // 2).astype(jnp.int32)
    wave = 2.0 * math.pi / box * freq.astype(jnp.float32)
    square = wave * wave
    inner = jnp.concatenate([square, square])
    total = square[:, None, None] + square[None, :, None] + inner[None, None, :]
    return 1.0 / (total + (8.0 * math.pi / box) ** 2)


def dft_tables(box):
    index = jnp.arange(box, dtype=jnp.int32)
    angle = 2.0 * math.pi / box * (index[:, None] * index[None, :] % box).astype(jnp.float32)
    return (jnp.cos(angle), jnp.sin(angle))


def swap_parts(block, box):
    return jnp.concatenate([block[..., box:], -block[..., :box]], axis=-1)


def poisson_solve(density, cosine, sine, kernel):
    box = density.shape[0]
    high = lax.Precision.HIGHEST
    forward_z = jnp.concatenate([cosine, -sine], axis=1)
    wave = jnp.dot(density.reshape(box * box, box), forward_z, precision=high).reshape(
        box, box, 2 * box
    )
    along = jnp.einsum("ky,xyw->xkw", cosine, wave, precision=high)
    across = jnp.einsum("ky,xyw->xkw", sine, wave, precision=high)
    wave = along + swap_parts(across, box)
    along = jnp.einsum("kx,xyw->kyw", cosine, wave, precision=high)
    across = jnp.einsum("kx,xyw->kyw", sine, wave, precision=high)
    wave = (along + swap_parts(across, box)) * kernel
    along = jnp.einsum("kx,xyw->kyw", cosine, wave, precision=high)
    across = jnp.einsum("kx,xyw->kyw", sine, wave, precision=high)
    wave = along - swap_parts(across, box)
    along = jnp.einsum("ky,xyw->xkw", cosine, wave, precision=high)
    across = jnp.einsum("ky,xyw->xkw", sine, wave, precision=high)
    wave = along - swap_parts(across, box)
    back_z = jnp.concatenate([cosine, -sine], axis=0)
    field = jnp.dot(wave.reshape(box * box, 2 * box), back_z, precision=high) / float(box**3)
    return field.reshape(box, box * box)


def body(orbitals, offsets, pair_list, pair_mask):
    orb_dev, box, flat = orbitals.shape
    count_x = lax.axis_size("dx")
    count_y = lax.axis_size("dy")
    place_x = lax.axis_index("dx")
    place_y = lax.axis_index("dy")
    base = (place_x * count_y + place_y) * orb_dev
    nearby = extended(orbitals[None, None], (("dx", 0), ("dy", 1)), 1)
    nearby = nearby.reshape(9 * orb_dev, box, flat)
    cosine, sine = dft_tables(box)
    kernel = kernel_tiled(box)

    def visit(slot, carry):
        own_total, outgoing = carry
        first = pair_list[slot, 0]
        second = pair_list[slot, 1]
        valid = pair_mask[slot].astype(jnp.float32)
        owner = second // orb_dev
        rel_x = (owner // count_y - place_x + 1) % count_x
        rel_y = (owner % count_y - place_y + 1) % count_y
        target = (rel_x * 3 + rel_y) * orb_dev + second % orb_dev
        local = first - base
        phi_first = lax.dynamic_index_in_dim(orbitals, local, 0, keepdims=False).astype(jnp.float32)
        phi_second = lax.dynamic_index_in_dim(nearby, target, 0, keepdims=False).astype(jnp.float32)
        move = offsets[first] - offsets[second]
        partner = shift_box(phi_second, move[0], move[1], move[2])
        density = phi_first * partner * valid
        potential = poisson_solve(density, cosine, sine, kernel)
        own_total = own_total.at[local].add(potential * partner)
        outgoing = outgoing.at[target].add(
            shift_box(potential * phi_first, -move[0], -move[1], -move[2])
        )
        return (own_total, outgoing)

    own_total = jnp.zeros((orb_dev, box, flat), jnp.float32)
    outgoing = jnp.zeros((9 * orb_dev, box, flat), jnp.float32)
    own_total, outgoing = lax.fori_loop(0, pair_list.shape[0], visit, (own_total, outgoing))
    outgoing = outgoing.reshape(3, 3, orb_dev, box, flat)
    arrived = outgoing[1, 1]
    for step, source in ((1, 2), (-1, 0)):
        arrived = arrived + shifted(outgoing[source, 1], "dx", step)
    for step, source in ((1, 2), (-1, 0)):
        arrived = arrived + shifted(outgoing[1, source], "dy", step)
    for step, source in ((1, 2), (-1, 0)):
        corners = shifted(outgoing[source, 0::2], "dx", step)
        for which, turn in ((0, -1), (1, 1)):
            arrived = arrived + shifted(corners[which], "dy", turn)
    return own_total + arrived


def solution(mesh):
    placed = (P(("dx", "dy"), None, None), P(), P(("dx", "dy"), None), P(("dx", "dy")))
    return jax.shard_map(
        body, mesh=mesh, in_specs=placed, out_specs=P(("dx", "dy"), None, None), check_vma=False
    )
```

profile of v0, /device:TPU:1, one launch (start us, length us, event | category | flops | bytes accessed | tf_op | source)
XLA Modules:
  0.0 795.5 jit_solution(7994754931239959957)
XLA Ops:
  0.0 4.2 collective-permute-start.1
  4.2 11.0 %collective-permute-done.1 = bf16[1,1,1,64,4096]{4,3,2,1,0:T(8,128)(2,1)S(1)} collective-permute-done((bf16[1,1,1,64,4096]{4,3,2,1,0:T(8,128)(2,1)}, bf16[1,1,1,64,4096]{4,3,2,1,0:T(8,128)(2,1)S(1)}, u32[]{:S(2)}, u32[]{:S(2)}) %collective-permute-start.1) | collective-permute-done | bytes 524320 | tf_op jit(solution)/shard_map/ppermute | solution.py:17
  15.2 11.9 %collective-permute-done = bf16[1,1,1,64,4096]{4,3,2,1,0:T(8,128)(2,1)S(1)} collective-permute-done((bf16[1,1,1,64,4096]{4,3,2,1,0:T(8,128)(2,1)}, bf16[1,1,1,64,4096]{4,3,2,1,0:T(8,128)(2,1)S(1)}, u32[]{:S(2)}, u32[]{:S(2)}) %collective-permute-start) | collective-permute-done | bytes 524320 | tf_op jit(solution)/shard_map/ppermute | solution.py:16
  32.5 34.2 %collective-permute-done.3 = bf16[3,1,1,64,4096]{4,3,2,1,0:T(8,128)(2,1)S(1)} collective-permute-done((bf16[3,1,1,64,4096]{4,3,2,1,0:T(8,128)(2,1)}, bf16[3,1,1,64,4096]{4,3,2,1,0:T(8,128)(2,1)S(1)}, u32[]{:S(2)}, u32[]{:S(2)}) %collective-permute-start.3) | collective-permute-done | bytes 1572896 | tf_op jit(solution)/shard_map/ppermute | solution.py:17
  66.8 3.7 pad_maximum_fusion
  70.4 4.8 broadcast_in_dim.70
  75.3 553.6 %while.22 = (s32[]{:T(128)}, f32[1,64,4096]{2,1,0:T(8,128)}, f32[9,64,4096]{2,1,0:T(8,128)}, s32[8,2]{0,1:T(2,128)S(1)}, s32[]{:T(128)}, /*index=5*/bf16[1,64,40...) while((s32[]{:T(128)}, f32[1,64,4096]{2,1,0:T(8,128)}, ...), condition=%wide.region_3.4_spmd.clone.clone, body=%wide.region_0.3_spmd.clone.clone.sunk | while | flops 4038606848 | bytes 101293472 | solution.py:122
  128.0 3.3 fusion.194
  132.2 3.9 fusion.196
  139.1 2.6 maximum_subtract_fusion.4
  141.8 3.3 fusion.198
  146.0 3.8 maximum_subtract_fusion.5
  158.7 4.7 add_select_fusion.6
  194.0 3.3 fusion.194
  198.2 3.9 fusion.196
  205.2 2.6 maximum_subtract_fusion.4
  207.8 3.3 fusion.198
  212.0 3.8 maximum_subtract_fusion.5
  224.7 4.6 add_select_fusion.6
  257.4 2.6 maximum_add_fusion.3
  260.0 3.3 fusion.194
  264.2 3.9 fusion.196
  271.2 2.6 maximum_subtract_fusion.4
  273.8 3.3 fusion.198
  278.0 3.8 maximum_subtract_fusion.5
  290.7 4.7 add_select_fusion.6
  326.1 3.3 fusion.194
  330.3 3.9 fusion.196
  337.2 2.6 maximum_subtract_fusion.4
  339.9 3.3 fusion.198
  344.1 3.8 maximum_subtract_fusion.5
  356.8 4.6 add_select_fusion.6
  392.1 3.3 fusion.194
  396.3 3.9 fusion.196
  403.2 2.6 maximum_subtract_fusion.4
  405.9 3.3 fusion.198
  410.1 3.8 maximum_subtract_fusion.5
  422.8 4.6 add_select_fusion.6
  458.0 3.3 fusion.194
  462.2 3.9 fusion.196
  469.2 2.6 maximum_subtract_fusion.4
  471.8 3.3 fusion.198
  476.0 3.8 maximum_subtract_fusion.5
  488.7 4.6 add_select_fusion.6
  524.0 3.3 fusion.194
  528.2 3.9 fusion.196
  535.1 2.6 maximum_subtract_fusion.4
  537.8 3.3 fusion.198
  542.0 3.8 maximum_subtract_fusion.5
  554.7 4.7 add_select_fusion.6
  587.4 2.6 maximum_add_fusion.3
  590.0 3.3 fusion.194
  594.2 3.9 fusion.196
  603.8 3.3 fusion.198
  608.0 3.8 maximum_subtract_fusion.5
  620.7 4.6 add_select_fusion.6
  639.8 38.8 %collective-permute-done.8 = f32[2,1,64,4096]{3,2,1,0:T(8,128)S(1)} collective-permute-done((f32[2,1,64,4096]{3,2,1,0:T(8,128)S(1)}, f32[2,1,64,4096]{3,2,1,0:T(8,128)S(1)}, u32[]{:S(2)}, u32[]{:S(2)}) %collective-permute-start.8) | collective-permute-done | bytes 2097184 | tf_op jit(solution)/shard_map/ppermute | solution.py:25
  678.8 46.0 %collective-permute-done.11 = f32[2,1,64,4096]{3,2,1,0:T(8,128)S(1)} collective-permute-done((f32[2,1,64,4096]{3,2,1,0:T(8,128)S(1)}, f32[2,1,64,4096]{3,2,1,0:T(8,128)S(1)}, u32[]{:S(2)}, u32[]{:S(2)}) %collective-permute-start.11) | collective-permute-done | bytes 2097184 | tf_op jit(solution)/shard_map/ppermute | solution.py:25
  724.8 21.9 %collective-permute-start.9 = (f32[1,64,4096]{2,1,0:T(8,128)S(1)}, f32[1,64,4096]{2,1,0:T(8,128)S(1)}, u32[]{:S(2)}, u32[]{:S(2)}) collective-permute-start(f32[1,64,4096]{2,1,0:T(8,128)S(1)} %get-tuple-element.652), channel_id=1, source_target_pairs={{0,7},{1,0},{2,1},{3,2},{4,3},{5,4},{6,5},{7,6},{8,15},{9,8},{10,9... | collective-permute-start | bytes 3145736 | tf_op jit(solution)/shard_map/ppermute | solution.py:25
  746.9 4.2 collective-permute-start.10
  752.9 16.3 %collective-permute-done.5 = f32[1,64,4096]{2,1,0:T(8,128)S(1)} collective-permute-done((f32[1,64,4096]{2,1,0:T(8,128)S(1)}, f32[1,64,4096]{2,1,0:T(8,128)S(1)}, u32[]{:S(2)}, u32[]{:S(2)}) %collective-permute-start.5) | collective-permute-done | bytes 1048608 | tf_op jit(solution)/shard_map/ppermute | solution.py:25
  769.2 5.0 collective-permute-done.10
  774.2 15.7 %collective-permute-done.12 = f32[1,64,4096]{2,1,0:T(8,128)S(1)} collective-permute-done((f32[1,64,4096]{2,1,0:T(8,128)S(1)}, f32[1,64,4096]{2,1,0:T(8,128)S(1)}, u32[]{:S(2)}, u32[]{:S(2)}) %collective-permute-start.12) | collective-permute-done | bytes 1048608 | tf_op jit(solution)/shard_map/ppermute | solution.py:25
  792.3 2.9 fusion.109
  (286 shorter events, 274.0 us)
Async XLA Ops:
  0.0 15.1 %collective-permute-start.1 = (bf16[1,1,1,64,4096]{4,3,2,1,0:T(8,128)(2,1)}, bf16[1,1,1,64,4096]{4,3,2,1,0:T(8,128)(2,1)S(1)}, u32[]{:S(2)}, u32[]{:S(2)}) collective-permute-start(bf16[1,1,1,64,4096]{4,3,2,1,0:T(8,128)(2,1)} %bitcast), channel_id=1, source_target_pairs={{8,0},{16,8},{24,16},{0,24},{9,1},{17,9},{25,17},{1,25},{10,2},{18... | collective-permute-start | bytes 1572872 | tf_op jit(solution)/shard_map/ppermute | solution.py:17
  4.2 22.9 %collective-permute-start = (bf16[1,1,1,64,4096]{4,3,2,1,0:T(8,128)(2,1)}, bf16[1,1,1,64,4096]{4,3,2,1,0:T(8,128)(2,1)S(1)}, u32[]{:S(2)}, u32[]{:S(2)}) collective-permute-start(bf16[1,1,1,64,4096]{4,3,2,1,0:T(8,128)(2,1)} %bitcast), channel_id=1, source_target_pairs={{0,8},{8,16},{16,24},{24,0},{1,9},{9,17},{17,25},{25,1},{2,10},{10... | collective-permute-start | bytes 1572872 | tf_op jit(solution)/shard_map/ppermute | solution.py:16
  29.5 37.3 %collective-permute-start.3 = (bf16[3,1,1,64,4096]{4,3,2,1,0:T(8,128)(2,1)}, bf16[3,1,1,64,4096]{4,3,2,1,0:T(8,128)(2,1)S(1)}, u32[]{:S(2)}, u32[]{:S(2)}) collective-permute-start(bf16[3,1,1,64,4096]{4,3,2,1,0:T(8,128)(2,1)} %pad_maximum_fusion.1), channel_id=1, source_target_pairs={{1,0},{2,1},{3,2},{4,3},{5,4},{6,5},{7,6},{0,7},{9,8},{10,9},{11,1... | collective-permute-start | bytes 4718600 | tf_op jit(solution)/shard_map/ppermute | solution.py:17
  31.0 35.8 %collective-permute-start.2 = (bf16[3,1,1,64,4096]{4,3,2,1,0:T(8,128)(2,1)}, bf16[3,1,1,64,4096]{4,3,2,1,0:T(8,128)(2,1)}, u32[]{:S(2)}, u32[]{:S(2)}) collective-permute-start(bf16[3,1,1,64,4096]{4,3,2,1,0:T(8,128)(2,1)} %pad_maximum_fusion.1), channel_id=1, source_target_pairs={{0,1},{1,2},{2,3},{3,4},{4,5},{5,6},{6,7},{7,0},{8,9},{9,10},{10,1... | collective-permute-start | bytes 4718600 | tf_op jit(solution)/shard_map/ppermute | solution.py:16
  70.4 4.9 copy-start.3
  70.4 4.9 copy-start.4
  70.4 4.9 copy-start.5
  70.4 4.9 copy-start.6
  157.4 1.2 copy-start
  163.4 1.0 copy-start.1
  223.5 1.2 copy-start
  229.3 1.0 copy-start.1
  289.5 1.2 copy-start
  295.4 1.0 copy-start.1
  355.6 1.2 copy-start
  361.4 1.0 copy-start.1
  421.5 1.2 copy-start
  427.4 1.0 copy-start.1
  487.5 1.2 copy-start
  493.3 1.0 copy-start.1
  553.4 1.2 copy-start
  559.3 1.0 copy-start.1
  619.5 1.2 copy-start
  625.3 1.0 copy-start.1
  631.4 47.2 %collective-permute-start.8 = (f32[2,1,64,4096]{3,2,1,0:T(8,128)S(1)}, f32[2,1,64,4096]{3,2,1,0:T(8,128)S(1)}, u32[]{:S(2)}, u32[]{:S(2)}) collective-permute-start(f32[2,1,64,4096]{3,2,1,0:T(8,128)S(1)} %get-tuple-element.650), channel_id=1, source_target_pairs={{0,8},{8,16},{16,24},{24,0},{1,9},{9,17},{17,25},{25,1},{2,10},{10... | collective-permute-start | bytes 6291464 | tf_op jit(solution)/shard_map/ppermute | solution.py:25
  632.5 92.3 %collective-permute-start.11 = (f32[2,1,64,4096]{3,2,1,0:T(8,128)S(1)}, f32[2,1,64,4096]{3,2,1,0:T(8,128)S(1)}, u32[]{:S(2)}, u32[]{:S(2)}) collective-permute-start(f32[2,1,64,4096]{3,2,1,0:T(8,128)S(1)} %get-tuple-element.651), channel_id=1, source_target_pairs={{0,24},{8,0},{16,8},{24,16},{1,25},{9,1},{17,9},{25,17},{2,26},{10... | collective-permute-start | bytes 6291464 | tf_op jit(solution)/shard_map/ppermute | solution.py:25
  637.2 109.7 %collective-permute-start.4 = (f32[1,64,4096]{2,1,0:T(8,128)S(1)}, f32[1,64,4096]{2,1,0:T(8,128)S(1)}, u32[]{:S(2)}, u32[]{:S(2)}) collective-permute-start(f32[1,64,4096]{2,1,0:T(8,128)S(1)} %get-tuple-element.646), channel_id=1, source_target_pairs={{0,8},{8,16},{16,24},{24,0},{1,9},{9,17},{17,25},{25,1},{2,10},{10... | collective-permute-start | bytes 3145736 | tf_op jit(solution)/shard_map/ppermute | solution.py:25
  637.3 113.9 %collective-permute-start.7 = (f32[1,64,4096]{2,1,0:T(8,128)S(1)}, f32[1,64,4096]{2,1,0:T(8,128)S(1)}, u32[]{:S(2)}, u32[]{:S(2)}) collective-permute-start(f32[1,64,4096]{2,1,0:T(8,128)S(1)} %get-tuple-element.647), channel_id=1, source_target_pairs={{0,7},{1,0},{2,1},{3,2},{4,3},{5,4},{6,5},{7,6},{8,15},{9,8},{10,9... | collective-permute-start | bytes 3145736 | tf_op jit(solution)/shard_map/ppermute | solution.py:25
  639.7 111.4 %collective-permute-start.6 = (f32[1,64,4096]{2,1,0:T(8,128)S(1)}, f32[1,64,4096]{2,1,0:T(8,128)S(1)}, u32[]{:S(2)}, u32[]{:S(2)}) collective-permute-start(f32[1,64,4096]{2,1,0:T(8,128)S(1)} %get-tuple-element.648), channel_id=1, source_target_pairs={{0,1},{1,2},{2,3},{3,4},{4,5},{5,6},{6,7},{7,0},{8,9},{9,10},{10,1... | collective-permute-start | bytes 3145736 | tf_op jit(solution)/shard_map/ppermute | solution.py:25
  678.6 90.5 %collective-permute-start.5 = (f32[1,64,4096]{2,1,0:T(8,128)S(1)}, f32[1,64,4096]{2,1,0:T(8,128)S(1)}, u32[]{:S(2)}, u32[]{:S(2)}) collective-permute-start(f32[1,64,4096]{2,1,0:T(8,128)S(1)} %get-tuple-element.649), channel_id=1, source_target_pairs={{0,24},{8,0},{16,8},{24,16},{1,25},{9,1},{17,9},{25,17},{2,26},{10... | collective-permute-start | bytes 3145736 | tf_op jit(solution)/shard_map/ppermute | solution.py:25
  724.8 67.5 %copy-start.2 = (f32[1,64,4096]{2,1,0:T(8,128)S(1)}, f32[1,64,4096]{2,1,0:T(8,128)}, u32[]{:S(2)}) copy-start(f32[1,64,4096]{2,1,0:T(8,128)} %get-tuple-element.500) | copy-start | bytes 3145732
  724.8 44.3 %collective-permute-start.9 = (f32[1,64,4096]{2,1,0:T(8,128)S(1)}, f32[1,64,4096]{2,1,0:T(8,128)S(1)}, u32[]{:S(2)}, u32[]{:S(2)}) collective-permute-start(f32[1,64,4096]{2,1,0:T(8,128)S(1)} %get-tuple-element.652), channel_id=1, source_target_pairs={{0,7},{1,0},{2,1},{3,2},{4,3},{5,4},{6,5},{7,6},{8,15},{9,8},{10,9... | collective-permute-start | bytes 3145736 | tf_op jit(solution)/shard_map/ppermute | solution.py:25
  746.9 27.3 %collective-permute-start.10 = (f32[1,64,4096]{2,1,0:T(8,128)S(1)}, f32[1,64,4096]{2,1,0:T(8,128)S(1)}, u32[]{:S(2)}, u32[]{:S(2)}) collective-permute-start(f32[1,64,4096]{2,1,0:T(8,128)S(1)} %get-tuple-element.653), channel_id=1, source_target_pairs={{0,1},{1,2},{2,3},{3,4},{4,5},{5,6},{6,7},{7,0},{8,9},{9,10},{10,1... | collective-permute-start | bytes 3145736 | tf_op jit(solution)/shard_map/ppermute | solution.py:25
  751.1 38.7 %collective-permute-start.12 = (f32[1,64,4096]{2,1,0:T(8,128)S(1)}, f32[1,64,4096]{2,1,0:T(8,128)S(1)}, u32[]{:S(2)}, u32[]{:S(2)}) collective-permute-start(f32[1,64,4096]{2,1,0:T(8,128)S(1)} %get-tuple-element.654), channel_id=1, source_target_pairs={{0,7},{1,0},{2,1},{3,2},{4,3},{5,4},{6,5},{7,6},{8,15},{9,8},{10,9... | collective-permute-start | bytes 3145736 | tf_op jit(solution)/shard_map/ppermute | solution.py:25
  751.1 41.2 %collective-permute-start.13 = (f32[1,64,4096]{2,1,0:T(8,128)S(1)}, f32[1,64,4096]{2,1,0:T(8,128)S(1)}, u32[]{:S(2)}, u32[]{:S(2)}) collective-permute-start(f32[1,64,4096]{2,1,0:T(8,128)S(1)} %get-tuple-element.655), channel_id=1, source_target_pairs={{0,1},{1,2},{2,3},{3,4},{4,5},{5,6},{6,7},{7,0},{8,9},{9,10},{10,1... | collective-permute-start | bytes 3145736 | tf_op jit(solution)/shard_map/ppermute | solution.py:25
where the time goes:
time: 802 us; the launch traced here: 795 us
  matrix products  225 us (28%)
  waiting for transfers between devices  182 us (23%)
  loops' own time  124 us (15%)
  other arithmetic  122 us (15%)
  local copies, waits for them, and re-layouts  102 us (13%)
  starting transfers between devices  40.5 us (5%)
    ppermute x10, waiting for transfers between devices, shifted(): return lax.ppermute(value, axis, pairs)  124 us
    another operation x1, loops' own time, body(): lax.fori_loop(0, pair_list.shape[0], visit, (own_total, outgoing))  124 us
    dot_general x16, matrix products, poisson_solve(): along = jnp.einsum('kx,xyw->kyw', cosine, wave, precision=high)  52.7 us
    dot_general x16, matrix products, poisson_solve(): along = jnp.einsum('ky,xyw->xkw', cosine, wave, precision=high)  51.5 us
    ppermute x2, waiting for transfers between devices, extended(): after = lax.ppermute(leading, axis, down)  45.2 us
    dot_general x16, matrix products, poisson_solve(): across = jnp.einsum('ky,xyw->xkw', sine, wave, precision=high)  43.6 us
    dot_general x16, matrix products, poisson_solve(): across = jnp.einsum('kx,xyw->kyw', sine, wave, precision=high)  43.6 us
    scatter-add x8, other arithmetic, visit(): own_total = own_total.at[local].add(potential * partner)  37.1 us
  transfers between devices with their start and end apart: 14, of which 9 were waited for; matrix products, arithmetic and copies ran while one was open for 0% of the time, Pallas kernels for 0%

commit v1 on v0

v1 whole, which is shorter than its diff:
```python
import functools
import math

import jax
import jax.numpy as jnp
import ml_dtypes
import numpy as np
from jax import lax
from jax.experimental import pallas as pl
from jax.experimental.pallas import tpu as pltpu
from jax.sharding import PartitionSpec as P

GROUP = 8


def basis(box):
    half = box // 2
    index = np.arange(box)
    freq = np.where(index <= half, index, index - half)
    angle = 2.0 * np.pi / box * ((freq[:, None] * index[None, :]) % box)
    rows = np.where(index[:, None] <= half, np.cos(angle), np.sin(angle))
    scale = np.where((index == 0) | (index == half), 1.0, math.sqrt(2.0)) / math.sqrt(box)
    return rows * scale[:, None], freq


def split_np(value):
    high = value.astype(ml_dtypes.bfloat16)
    low = (value - high.astype(np.float64)).astype(ml_dtypes.bfloat16)
    return high, low


def left_table(matrix):
    high, low = split_np(matrix)
    return np.block([[high, high], [low, np.zeros_like(low)]])


def right_table(matrix):
    high, low = split_np(np.kron(np.eye(2), matrix))
    return np.block([[high, low], [high, np.zeros_like(low)]])


def tables(box):
    rows, freq = basis(box)
    wave = 2.0 * np.pi / box * freq
    square = (wave * wave).astype(np.float32)
    column = square[:, None] + np.zeros((1, 2 * box), np.float32)
    lane = np.concatenate([square, square])[None, :] + np.zeros((8, 1), np.float32)
    return (
        left_table(rows),
        left_table(rows.T),
        right_table(rows.T),
        right_table(rows),
        column,
        lane,
    )


def split(value):
    high = value.astype(jnp.bfloat16)
    low = (value - high.astype(jnp.float32)).astype(jnp.bfloat16)
    return high, low


def apply_left(table, tiles):
    box = tiles[0].shape[0]
    high, low = split(jnp.concatenate(tiles, axis=1))
    both = jnp.concatenate([high, low], axis=0)
    out = jnp.dot(table, both, preferred_element_type=jnp.float32)
    out = out[:box] + out[box:]
    return [out[:, 128 * i : 128 * (i + 1)] for i in range(len(tiles))]


def apply_right(table, tiles):
    box, lanes = tiles[0].shape
    high, low = split(jnp.concatenate(tiles, axis=0))
    both = jnp.concatenate([high, low], axis=1)
    out = jnp.dot(both, table, preferred_element_type=jnp.float32)
    out = out[:, :lanes] + out[:, lanes:]
    return [out[box * i : box * (i + 1)] for i in range(len(tiles))]


def placing(box, which, move_z):
    rows = lax.broadcasted_iota(jnp.int32, (4 * box, 8 * box), 0)
    cols = lax.broadcasted_iota(jnp.int32, (4 * box, 8 * box), 1)
    keep = (rows // box == cols // (2 * box)) & (rows % box == cols % box + move_z)
    if which is not None:
        keep = keep & ((cols // box) % 2 == which)
    return jnp.where(keep, 1.0, 0.0).astype(jnp.bfloat16)


def kernel(pairs, has_prev, box, *refs):
    units = 2 * pairs
    info, left_f, left_i, right_f, right_i, column, lane_sq, own = refs[:8]
    others = refs[8 : 8 + units]
    rest = refs[8 + units :]
    if has_prev:
        prev, rest = rest[0], rest[1:]
    out, staged, partner, work, total, phi, green = rest
    chunks = box // 4
    flat_rows = box * box

    lane = lax.broadcasted_iota(jnp.int32, (box, 2 * box), 1)
    low_half = lane < box

    staged[...] = jnp.zeros_like(staged)
    total[...] = jnp.zeros_like(total)
    place_own = placing(box, None, 0)

    def prepare(j, carry):
        part = own[:, pl.ds(pl.multiple_of(j * 4 * box, 4 * box), 4 * box)]
        res = jnp.dot(part, place_own, preferred_element_type=jnp.float32)
        for i in range(4):
            start = pl.multiple_of((4 * j + i) * box, box)
            phi[pl.ds(start, box), :] = res[:, 2 * box * i : 2 * box * (i + 1)]
            wx = column[pl.ds(4 * j + i, 1), :]
            sq = column[...] + lane_sq[0:1, :] + wx + (8.0 * math.pi / box) ** 2
            green[pl.ds(start, box), :] = 1.0 / sq
        return carry

    lax.fori_loop(0, chunks, prepare, 0)

    def one_pair(p, carry):
        unit_a, unit_b = 2 * p, 2 * p + 1
        count_a = info[unit_a, 3]
        count_b = info[unit_b, 3]

        @pl.when(count_a + count_b > 0)
        def _():
            place = jnp.concatenate(
                [placing(box, 0, info[unit_a, 2]), placing(box, 1, info[unit_b, 2])], axis=0
            )
            for q in range(pairs):

                @pl.when(p == q)
                def _():
                    def stage(j, inner):
                        here = pl.ds(pl.multiple_of(j * 4 * box, 4 * box), 4 * box)
                        part = jnp.concatenate(
                            [others[2 * q][:, here], others[2 * q + 1][:, here]], axis=1
                        )
                        res = jnp.dot(part, place, preferred_element_type=jnp.float32)
                        for i in range(4):
                            start = pl.multiple_of((4 * j + i) * 2 * box + box // 2, box // 2)
                            staged[pl.ds(start, box), :] = res[:, 2 * box * i : 2 * box * (i + 1)]
                        return inner

                    lax.fori_loop(0, chunks, stage, 0)

            def fetch(y, unit):
                source = y + info[unit, 1]
                inside = (source >= 0) & (source < box)
                row = jnp.clip(source, 0, box - 1) * 2 * box + box // 2 + info[unit, 0]
                return staged[pl.ds(row, box), :] * jnp.where(inside, 1.0, 0.0)

            def forward(g, inner):
                tiles = []
                for i in range(GROUP):
                    y = g * GROUP + i
                    start = pl.multiple_of(y * box, box)
                    moved = jnp.where(low_half, fetch(y, unit_a), fetch(y, unit_b))
                    partner[pl.ds(start, box), :] = moved
                    tiles.append(moved * phi[pl.ds(start, box), :])
                tiles = apply_right(right_f[...], apply_left(left_f[...], tiles))
                for i in range(GROUP):
                    start = pl.multiple_of((g * GROUP + i) * box, box)
                    work[pl.ds(start, box), :] = tiles[i]
                return inner

            lax.fori_loop(0, box // GROUP, forward, 0)

            def middle(g, inner):
                tiles = []
                for i in range(GROUP):
                    tiles.append(work[pl.ds(g * GROUP + i, box, stride=box), :])
                tiles = apply_left(left_f[...], tiles)
                for i in range(GROUP):
                    start = pl.multiple_of((g * GROUP + i) * box, box)
                    tiles[i] = tiles[i] * green[pl.ds(start, box), :]
                tiles = apply_left(left_i[...], tiles)
                for i in range(GROUP):
                    work[pl.ds(g * GROUP + i, box, stride=box), :] = tiles[i]
                return inner

            lax.fori_loop(0, box // GROUP, middle, 0)
            weight = jnp.where(low_half, count_a.astype(jnp.float32), count_b.astype(jnp.float32))

            def back(g, inner):
                tiles = []
                for i in range(GROUP):
                    start = pl.multiple_of((g * GROUP + i) * box, box)
                    tiles.append(work[pl.ds(start, box), :])
                tiles = apply_left(left_i[...], apply_right(right_i[...], tiles))
                for i in range(GROUP):
                    start = pl.multiple_of((g * GROUP + i) * box, box)
                    here = pl.ds(start, box)
                    total[here, :] = total[here, :] + tiles[i] * partner[here, :] * weight
                return inner

            lax.fori_loop(0, box // GROUP, back, 0)

        return carry

    lax.fori_loop(0, pairs, one_pair, 0)

    def finish(j, carry):
        even = total[pl.ds(pl.multiple_of(2 * j * box, box), box), :]
        odd = total[pl.ds(pl.multiple_of((2 * j + 1) * box, box), box), :]
        even = even + pltpu.roll(even, box, 1)
        odd = odd + pltpu.roll(odd, box, 1)
        res = jnp.where(low_half, even, odd)
        here = pl.ds(pl.multiple_of(j * 2 * box, 2 * box), 2 * box)
        if has_prev:
            res = res + prev[:, here]
        out[:, here] = res
        return carry

    lax.fori_loop(0, box // 2, finish, 0)


def pair_sum(info, consts, own, others, prev=None):
    box, flat = own.shape
    pairs = len(others) // 2
    vmem = pl.BlockSpec(memory_space=pltpu.VMEM)
    operands = [info, *consts, own, *others] + ([] if prev is None else [prev])
    specs = [pl.BlockSpec(memory_space=pltpu.SMEM)] + [vmem] * (len(operands) - 1)
    rows = box * box
    macs = pairs * 7 * 4096 * 65536
    return pl.pallas_call(
        functools.partial(kernel, pairs, prev is not None, box),
        out_shape=jax.ShapeDtypeStruct((box, flat), jnp.float32),
        in_specs=specs,
        out_specs=vmem,
        scratch_shapes=[pltpu.VMEM((2 * rows, 2 * box), jnp.float32)]
        + [pltpu.VMEM((rows, 2 * box), jnp.float32)] * 5,
        compiler_params=pltpu.CompilerParams(vmem_limit_bytes=48 * 1024 * 1024),
        cost_estimate=pl.CostEstimate(
            flops=2 * macs, bytes_accessed=pairs * 2 * rows * box * 2, transcendentals=0
        ),
    )(*operands)


def shifted(value, axis, steps):
    count = lax.axis_size(axis)
    pairs = [(source, (source + steps) % count) for source in range(count)]
    return lax.ppermute(value, axis, pairs)


def body(orbitals, offsets, pair_list, pair_mask):
    box = orbitals.shape[1]
    count_x = lax.axis_size("dx")
    count_y = lax.axis_size("dy")
    place_x = lax.axis_index("dx")
    place_y = lax.axis_index("dy")
    me = place_x * count_y + place_y
    own = orbitals[0]
    near = {(0, 0): own}
    for i in (-1, 1):
        near[i, 0] = shifted(own, "dx", -i)
    for i in (0, -1, 1):
        for j in (-1, 1):
            near[i, j] = shifted(near[i, 0], "dy", -j)

    cells = [(i, j) for i in (-1, 0, 1) for j in (-1, 0, 1)]
    mates = jnp.stack(
        [((place_x + i) % count_x) * count_y + (place_y + j) % count_y for i, j in cells]
    )
    second = pair_list[:, 1]
    mine = jnp.sum(
        jnp.where(second[None, :] == mates[:, None], pair_mask[None, :], 0), axis=1
    )
    every = lax.all_gather(mine, ("dx", "dy"), axis=0, tiled=False)
    every = every.reshape(count_x * count_y, len(cells))
    theirs = every[mates, len(cells) - 1 - jnp.arange(len(cells))]
    counts = mine + theirs
    move = offsets[me][None, :] - offsets[mates]
    info = jnp.concatenate([move, counts[:, None]], axis=1).astype(jnp.int32)
    nothing = jnp.zeros((1, 4), jnp.int32)
    info = jnp.concatenate([info, nothing], axis=0)

    consts = tuple(jnp.asarray(t) for t in tables(box))
    order = [(0, 0), None, (0, -1), (0, 1), (-1, 0), (1, 0), (-1, -1), (-1, 1), (1, -1), (1, 1)]
    pick = np.array([len(cells) if c is None else cells.index(c) for c in order])
    others = [own if c is None else near[c] for c in order]
    return pair_sum(info[pick], consts, own, others)[None]


def solution(mesh):
    placed = (P(("dx", "dy"), None, None), P(), P(("dx", "dy"), None), P(("dx", "dy")))
    return jax.shard_map(
        body, mesh=mesh, in_specs=placed, out_specs=P(("dx", "dy"), None, None), check_vma=False
    )
```

time: 802 us -> 163 us (0.20)
  the two profiles are of different devices: /device:TPU:1 before, /device:TPU:7 now
where the time goes in v1:
time: 163 us; the launch traced here: 161 us
  Pallas kernels  82.8 us (51%)
  blocking collectives  44.3 us (27%)
  waiting for transfers between devices  18.4 us (11%)
  starting transfers between devices  11.3 us (7%)
  local copies, waits for them, and re-layouts  4.04 us (2%)
    pallas_call x1, Pallas kernels, pair_sum(): pl.pallas_call(functools.partial(kernel, pairs, prev is not None, box), o...  82.8 us
    unnamed x1, blocking collectives  44.3 us
    ppermute x8, waiting for transfers between devices, shifted(): return lax.ppermute(value, axis, pairs)  18.4 us
    ppermute x8, starting transfers between devices, shifted(): return lax.ppermute(value, axis, pairs)  11.3 us
  transfers between devices with their start and end apart: 8, of which 3 were waited for; matrix products, arithmetic and copies ran while one was open for 2% of the time, Pallas kernels for 0%

profile of v1, /device:TPU:7, one launch (start us, length us, event | category | flops | bytes accessed | tf_op | source)
XLA Modules:
  0.0 161.3 jit_solution(6621349162590188736)
XLA Ops:
  0.0 3.3 %collective-permute-start.3 = (bf16[64,4096]{1,0:T(8,128)(2,1)}, bf16[64,4096]{1,0:T(8,128)(2,1)S(1)}, u32[]{:S(2)}, u32[]{:S(2)}) collective-permute-start(bf16[64,4096]{1,0:T(8,128)(2,1)} %bitcast.28), channel_id=1, source_target_pairs={{0,24},{8,0},{16,8},{24,16},{1,25},{9,1},{17,9},{25,17},{2,26},{10... | collective-permute-start | bytes 1572872 | tf_op jit(solution)/shard_map/ppermute | solution.py:245
  3.3 0.0 collective-permute-start.2
  3.3 1.0 collective-permute-start.1
  4.3 1.7 %collective-permute-start = (bf16[64,4096]{1,0:T(8,128)(2,1)}, bf16[64,4096]{1,0:T(8,128)(2,1)S(1)}, u32[]{:S(2)}, u32[]{:S(2)}) collective-permute-start(bf16[64,4096]{1,0:T(8,128)(2,1)} %bitcast.31), channel_id=1, source_target_pairs={{0,1},{1,2},{2,3},{3,4},{4,5},{5,6},{6,7},{7,0},{8,9},{9,10},{10,1... | collective-permute-start | bytes 1572872 | tf_op jit(solution)/shard_map/ppermute | solution.py:245
  6.0 0.0 copy-start.10
  6.0 0.0 copy-start.9
  6.0 0.0 copy-start.7
  6.0 0.0 copy-start
  6.1 0.6 copy-done.7
  6.7 0.1 copy.20
  6.8 0.2 dynamic-slice_reduce_fusion
  7.0 0.0 copy-done.10
  7.0 0.1 stack.69
  7.1 0.0 copy-done.9
  7.1 0.1 select_reduce_fusion
  7.2 0.2 dynamic-update-slice
  7.4 44.3 %all-reduce.1 = s32[288]{0:T(512)S(1)} all-reduce(s32[288]{0:T(512)S(1)} %dynamic-update-slice), channel_id=2, replica_groups=mesh['dx'=4,'dy'=8] {'dx','dy'}, use_global_device_ids=true, to_apply=%add.1 | all-reduce | flops 288 | bytes 2304
  51.7 0.1 reshape.407
  51.8 0.1 stack.59
  51.9 0.0 copy-start.2
  51.9 0.0 copy-start.5
  52.0 0.7 gather_fusion.1
  52.7 0.0 copy-start.1
  52.7 0.1 copy.21
  52.8 0.0 collective-permute-done.3.refs_13_
  52.8 0.9 collective-permute-start.7
  53.7 1.7 %collective-permute-start.6 = (bf16[64,4096]{1,0:T(8,128)(2,1)S(1)}, bf16[64,4096]{1,0:T(8,128)(2,1)}, u32[]{:S(2)}, u32[]{:S(2)}) collective-permute-start(bf16[64,4096]{1,0:T(8,128)(2,1)S(1)} %collective-permute-done.3.refs_13_), channel_id=1, source_target_pairs={{0,1},{1,2},{2,3},{3,4},{4,5},{5,6},{6,7},{7,0},{8,9},{9,10},{10,1... | collective-permute-start | bytes 1572872 | tf_op jit(solution)/shard_map/ppermute | solution.py:245
  55.4 0.0 collective-permute-done.2.refs_12_
  55.4 0.0 collective-permute-start.5
  55.4 0.0 collective-permute-done.1.refs_11_
  55.4 2.6 %collective-permute-start.4 = (bf16[64,4096]{1,0:T(8,128)(2,1)S(1)}, bf16[64,4096]{1,0:T(8,128)(2,1)}, u32[]{:S(2)}, u32[]{:S(2)}) collective-permute-start(bf16[64,4096]{1,0:T(8,128)(2,1)S(1)} %collective-permute-done.2.refs_12_), channel_id=1, source_target_pairs={{0,1},{1,2},{2,3},{3,4},{4,5},{5,6},{6,7},{7,0},{8,9},{9,10},{10,1... | collective-permute-start | bytes 1572872 | tf_op jit(solution)/shard_map/ppermute | solution.py:245
  58.1 0.6 gather_fusion
  58.6 0.1 pad_add_fusion
  58.7 0.0 copy-start.8
  58.7 0.6 copy-done.8
  59.4 0.0 copy-start.3
  59.4 0.0 copy-start.4
  59.4 0.0 copy-start.6
  59.4 0.6 gather_fusion.2
  60.0 0.0 collective-permute-done.refs_10_
  60.0 7.1 %collective-permute-done.7.refs_17_ = bf16[64,4096]{1,0:T(8,128)(2,1)S(1)} collective-permute-done((bf16[64,4096]{1,0:T(8,128)(2,1)S(1)}, bf16[64,4096]{1,0:T(8,128)(2,1)S(1)}, u32[]{:S(2)}, u32[]{:S(2)}) %collective-permute-start.7) | collective-permute-done | bytes 524320 | tf_op jit(solution)/shard_map/ppermute | solution.py:245
  67.1 0.2 collective-permute-done.6.refs_16_
  67.2 11.2 %collective-permute-done.5.refs_15_ = bf16[64,4096]{1,0:T(8,128)(2,1)} collective-permute-done((bf16[64,4096]{1,0:T(8,128)(2,1)S(1)}, bf16[64,4096]{1,0:T(8,128)(2,1)}, u32[]{:S(2)}, u32[]{:S(2)}) %collective-permute-start.5) | collective-permute-done | bytes 524320 | tf_op jit(solution)/shard_map/ppermute | solution.py:245
  78.4 0.0 collective-permute-done.4.refs_14_
  78.4 0.0 copy-done
  78.4 0.0 copy-done.2
  78.4 0.0 copy-done.5
  78.4 0.0 copy-done.1
  78.4 0.0 copy-done.3
  78.5 0.0 copy-done.4
  78.5 0.0 copy-done.6
  78.5 82.8 %shard_map.118 = f32[64,4096]{1,0:T(8,128)} custom-call(s32[10,4]{1,0:T(8,128)S(1)} %gather_fusion.2, bf16[128,128]{1,0:T(8,128)(2,1)S(1)} %copy-done.5, bf16[128,128]{1,0:T(8,128)(2,1)S(1)} %copy-done.4, bf16[256,256]{1,0:T(8,128)(2,1)S(1)} %copy-done.2, bf16[256,256]{1,0:T(8,128)(2,1)S(1)} %copy-done.1, f32[64,128]{1,0:T(8,128)S(1)} %copy-done.3, ...), custom_call_target="tpu_custom_call" | custom-call | flops 18790481920 | bytes 5242880 | tf_op jit(solution)/shard_map/pallas_call | solution.py:228
  (8 shorter events, 0.0 us)
Async XLA Ops:
  0.0 52.8 %collective-permute-start.3 = (bf16[64,4096]{1,0:T(8,128)(2,1)}, bf16[64,4096]{1,0:T(8,128)(2,1)S(1)}, u32[]{:S(2)}, u32[]{:S(2)}) collective-permute-start(bf16[64,4096]{1,0:T(8,128)(2,1)} %bitcast.28), channel_id=1, source_target_pairs={{0,24},{8,0},{16,8},{24,16},{1,25},{9,1},{17,9},{25,17},{2,26},{10... | collective-permute-start | bytes 1572872 | tf_op jit(solution)/shard_map/ppermute | solution.py:245
  3.3 52.1 %collective-permute-start.2 = (bf16[64,4096]{1,0:T(8,128)(2,1)}, bf16[64,4096]{1,0:T(8,128)(2,1)S(1)}, u32[]{:S(2)}, u32[]{:S(2)}) collective-permute-start(bf16[64,4096]{1,0:T(8,128)(2,1)} %bitcast.29), channel_id=1, source_target_pairs={{0,8},{8,16},{16,24},{24,0},{1,9},{9,17},{17,25},{25,1},{2,10},{10... | collective-permute-start | bytes 1572872 | tf_op jit(solution)/shard_map/ppermute | solution.py:245
  3.3 52.1 %collective-permute-start.1 = (bf16[64,4096]{1,0:T(8,128)(2,1)}, bf16[64,4096]{1,0:T(8,128)(2,1)S(1)}, u32[]{:S(2)}, u32[]{:S(2)}) collective-permute-start(bf16[64,4096]{1,0:T(8,128)(2,1)} %bitcast.30), channel_id=1, source_target_pairs={{0,7},{1,0},{2,1},{3,2},{4,3},{5,4},{6,5},{7,6},{8,15},{9,8},{10,9... | collective-permute-start | bytes 1572872 | tf_op jit(solution)/shard_map/ppermute | solution.py:245
  4.3 55.7 %collective-permute-start = (bf16[64,4096]{1,0:T(8,128)(2,1)}, bf16[64,4096]{1,0:T(8,128)(2,1)S(1)}, u32[]{:S(2)}, u32[]{:S(2)}) collective-permute-start(bf16[64,4096]{1,0:T(8,128)(2,1)} %bitcast.31), channel_id=1, source_target_pairs={{0,1},{1,2},{2,3},{3,4},{4,5},{5,6},{6,7},{7,0},{8,9},{9,10},{10,1... | collective-permute-start | bytes 1572872 | tf_op jit(solution)/shard_map/ppermute | solution.py:245
  6.0 1.0 copy-start.10
  6.0 1.1 copy-start.9
  6.0 0.7 copy-start.7
  6.0 72.4 %copy-start = (bf16[1,64,4096]{2,1,0:T(8,128)(2,1)S(1)}, bf16[1,64,4096]{2,1,0:T(8,128)(2,1)}, u32[]{:S(2)}) copy-start(bf16[1,64,4096]{2,1,0:T(8,128)(2,1)} %param.12) | copy-start | bytes 1572868
  51.9 26.5 %copy-start.2 = (bf16[256,256]{1,0:T(8,128)(2,1)S(1)}, bf16[256,256]{1,0:T(8,128)(2,1)}, u32[]{:S(2)}) copy-start(bf16[256,256]{1,0:T(8,128)(2,1)} %constant.105.clone.refs_3_) | copy-start | bytes 393220
  51.9 26.5 %copy-start.5 = (bf16[128,128]{1,0:T(8,128)(2,1)S(1)}, bf16[128,128]{1,0:T(8,128)(2,1)}, u32[]{:S(2)}) copy-start(bf16[128,128]{1,0:T(8,128)(2,1)} %constant.103.clone.refs_1_) | copy-start | bytes 98308
  52.7 25.8 %copy-start.1 = (bf16[256,256]{1,0:T(8,128)(2,1)S(1)}, bf16[256,256]{1,0:T(8,128)(2,1)}, u32[]{:S(2)}) copy-start(bf16[256,256]{1,0:T(8,128)(2,1)} %constant.106.clone.refs_4_) | copy-start | bytes 393220
  52.8 14.3 %collective-permute-start.7 = (bf16[64,4096]{1,0:T(8,128)(2,1)S(1)}, bf16[64,4096]{1,0:T(8,128)(2,1)S(1)}, u32[]{:S(2)}, u32[]{:S(2)}) collective-permute-start(bf16[64,4096]{1,0:T(8,128)(2,1)S(1)} %collective-permute-done.3.refs_13_), channel_id=1, source_target_pairs={{0,7},{1,0},{2,1},{3,2},{4,3},{5,4},{6,5},{7,6},{8,15},{9,8},{10,9... | collective-permute-start | bytes 1572872 | tf_op jit(solution)/shard_map/ppermute | solution.py:245
  53.7 13.5 %collective-permute-start.6 = (bf16[64,4096]{1,0:T(8,128)(2,1)S(1)}, bf16[64,4096]{1,0:T(8,128)(2,1)}, u32[]{:S(2)}, u32[]{:S(2)}) collective-permute-start(bf16[64,4096]{1,0:T(8,128)(2,1)S(1)} %collective-permute-done.3.refs_13_), channel_id=1, source_target_pairs={{0,1},{1,2},{2,3},{3,4},{4,5},{5,6},{6,7},{7,0},{8,9},{9,10},{10,1... | collective-permute-start | bytes 1572872 | tf_op jit(solution)/shard_map/ppermute | solution.py:245
  55.4 23.0 %collective-permute-start.5 = (bf16[64,4096]{1,0:T(8,128)(2,1)S(1)}, bf16[64,4096]{1,0:T(8,128)(2,1)}, u32[]{:S(2)}, u32[]{:S(2)}) collective-permute-start(bf16[64,4096]{1,0:T(8,128)(2,1)S(1)} %collective-permute-done.2.refs_12_), channel_id=1, source_target_pairs={{0,7},{1,0},{2,1},{3,2},{4,3},{5,4},{6,5},{7,6},{8,15},{9,8},{10,9... | collective-permute-start | bytes 1572872 | tf_op jit(solution)/shard_map/ppermute | solution.py:245
  55.4 23.0 %collective-permute-start.4 = (bf16[64,4096]{1,0:T(8,128)(2,1)S(1)}, bf16[64,4096]{1,0:T(8,128)(2,1)}, u32[]{:S(2)}, u32[]{:S(2)}) collective-permute-start(bf16[64,4096]{1,0:T(8,128)(2,1)S(1)} %collective-permute-done.2.refs_12_), channel_id=1, source_target_pairs={{0,1},{1,2},{2,3},{3,4},{4,5},{5,6},{6,7},{7,0},{8,9},{9,10},{10,1... | collective-permute-start | bytes 1572872 | tf_op jit(solution)/shard_map/ppermute | solution.py:245
  58.7 0.7 copy-start.8
  59.4 19.1 %copy-start.3 = (f32[64,128]{1,0:T(8,128)S(1)}, f32[64,128]{1,0:T(8,128)}, u32[]{:S(2)}) copy-start(f32[64,128]{1,0:T(8,128)} %constant.107.clone.refs_5_) | copy-start | bytes 98308
  59.4 19.1 %copy-start.4 = (bf16[128,128]{1,0:T(8,128)(2,1)S(1)}, bf16[128,128]{1,0:T(8,128)(2,1)}, u32[]{:S(2)}) copy-start(bf16[128,128]{1,0:T(8,128)(2,1)} %constant.104.clone.refs_2_) | copy-start | bytes 98308
  59.4 19.1 %copy-start.6 = (f32[8,128]{1,0:T(8,128)S(1)}, f32[8,128]{1,0:T(8,128)}, u32[]{:S(2)}) copy-start(f32[8,128]{1,0:T(8,128)} %constant.108.clone.refs_6_) | copy-start | bytes 12292

commit v2 on v1

v2 whole, which is shorter than its diff:
```python
import functools
import math

import jax
import jax.numpy as jnp
import ml_dtypes
import numpy as np
from jax import lax
from jax.experimental import pallas as pl
from jax.experimental.pallas import tpu as pltpu
from jax.sharding import PartitionSpec as P

GROUP = 8
CELLS = [(i, j) for i in (-1, 0, 1) for j in (-1, 0, 1)]
SLOTS = [cell for cell in CELLS if cell != (0, 0)]
ORDER = [(0, 0), (0, 0), (-1, 0), (1, 0), (0, -1), (0, 1), (-1, -1), (-1, 1), (1, -1), (1, 1)]
PAIRS = len(ORDER) // 2


def basis(box):
    half = box // 2
    index = np.arange(box)
    freq = np.where(index <= half, index, index - half)
    angle = 2.0 * np.pi / box * ((freq[:, None] * index[None, :]) % box)
    rows = np.where(index[:, None] <= half, np.cos(angle), np.sin(angle))
    scale = np.where((index == 0) | (index == half), 1.0, math.sqrt(2.0)) / math.sqrt(box)
    return rows * scale[:, None], freq


def split_np(value):
    high = value.astype(ml_dtypes.bfloat16)
    low = (value - high.astype(np.float64)).astype(ml_dtypes.bfloat16)
    return high, low


def left_table(matrix):
    high, low = split_np(matrix)
    return np.block([[high, high], [low, np.zeros_like(low)]])


def right_table(matrix):
    high, low = split_np(np.kron(np.eye(2), matrix))
    return np.block([[high, low], [high, np.zeros_like(low)]])


def tables(box):
    rows, freq = basis(box)
    wave = 2.0 * np.pi / box * freq
    square = (wave * wave).astype(np.float32)
    column = square[:, None] + np.zeros((1, 2 * box), np.float32)
    lane = np.concatenate([square, square])[None, :] + np.zeros((8, 1), np.float32)
    return (
        left_table(rows),
        left_table(rows.T),
        right_table(rows.T),
        right_table(rows),
        column,
        lane,
    )


def split(value):
    high = value.astype(jnp.bfloat16)
    low = (value - high.astype(jnp.float32)).astype(jnp.bfloat16)
    return high, low


def apply_left(table, tiles):
    box = tiles[0].shape[0]
    high, low = split(jnp.concatenate(tiles, axis=1))
    both = jnp.concatenate([high, low], axis=0)
    out = jnp.dot(table, both, preferred_element_type=jnp.float32)
    out = out[:box] + out[box:]
    return [out[:, 128 * i : 128 * (i + 1)] for i in range(len(tiles))]


def apply_right(table, tiles):
    box, lanes = tiles[0].shape
    high, low = split(jnp.concatenate(tiles, axis=0))
    both = jnp.concatenate([high, low], axis=1)
    out = jnp.dot(both, table, preferred_element_type=jnp.float32)
    out = out[:, :lanes] + out[:, lanes:]
    return [out[box * i : box * (i + 1)] for i in range(len(tiles))]


def placing(box, which, move_z):
    rows = lax.broadcasted_iota(jnp.int32, (4 * box, 8 * box), 0)
    cols = lax.broadcasted_iota(jnp.int32, (4 * box, 8 * box), 1)
    keep = (rows // box == cols // (2 * box)) & (rows % box == cols % box + move_z)
    if which is not None:
        keep = keep & ((cols // box) % 2 == which)
    return jnp.where(keep, 1.0, 0.0).astype(jnp.bfloat16)


def kernel(count_x, count_y, box, *refs):
    offsets, pair_list, pair_mask, left_f, left_i, right_f, right_i, column, lane_sq, own = refs[:10]
    out, staged, partner, work, total, phi, green = refs[10:17]
    tally, weights, moves, landed, landed_tally = refs[17:22]
    send_sem, recv_sem, tally_send, tally_recv = refs[22:]
    chunks = box // 4
    pitch = box + 8

    place_x = lax.axis_index("dx")
    place_y = lax.axis_index("dy")

    def domain(i, j):
        return lax.rem(place_x + i + count_x, count_x), lax.rem(place_y + j + count_y, count_y)

    def owner(i, j):
        x, y = domain(i, j)
        return x * count_y + y

    def target(i, j):
        x, y = domain(i, j)
        return {"dx": x} if j == 0 else {"dy": y}

    barrier = pltpu.get_barrier_semaphore()
    for step in ((1, 0), (-1, 0), (0, 1), (0, -1)):
        pl.semaphore_signal(
            barrier, inc=1, device_id=target(*step), device_id_type=pl.DeviceIdType.MESH
        )

    tally[...] = jnp.zeros_like(tally)
    for row, (i, j) in enumerate(CELLS):
        number = jnp.int32(0)
        for slot in range(pair_mask.shape[0]):
            same = pair_list[slot, 1] == owner(i, j)
            number = number + jnp.where(same, pair_mask[slot], 0)
        tally[row : row + 1, :] = jnp.full((1, 2 * box), 1.0, jnp.float32) * number.astype(
            jnp.float32
        )
    mine = owner(0, 0)
    for unit, cell in enumerate(ORDER):
        for axis in range(3):
            moves[unit, axis] = offsets[mine, axis] - offsets[owner(*cell), axis]

    pl.semaphore_wait(barrier, 4)

    def copies(source, i, j):
        slot = SLOTS.index((source[0] - i, source[1] - j))
        block, number = (own, tally)
        if source != (0, 0):
            block = landed.at[SLOTS.index(source)]
            number = landed_tally.at[SLOTS.index(source)]
        made = []
        for src, dst, send, recv in (
            (number, landed_tally, tally_send, tally_recv),
            (block, landed, send_sem, recv_sem),
        ):
            made.append(
                pltpu.make_async_remote_copy(
                    src_ref=src,
                    dst_ref=dst.at[slot],
                    send_sem=send.at[slot],
                    recv_sem=recv.at[slot],
                    device_id=target(i, j),
                    device_id_type=pl.DeviceIdType.MESH,
                )
            )
        return made

    first = [copies((0, 0), *step) for step in ((1, 0), (-1, 0), (0, 1), (0, -1))]
    relay = [copies((i, 0), 0, j) for i in (-1, 1) for j in (1, -1)]
    arrive = {(-1, 0): first[0], (1, 0): first[1], (0, -1): first[2], (0, 1): first[3]}
    arrive.update({(-1, -1): relay[0], (-1, 1): relay[1], (1, -1): relay[2], (1, 1): relay[3]})
    for pair in first:
        for copy in pair:
            copy.start()

    lane = lax.broadcasted_iota(jnp.int32, (box, 2 * box), 1)
    low_half = lane < box

    staged[...] = jnp.zeros_like(staged)
    total[...] = jnp.zeros_like(total)
    place_own = placing(box, None, 0)

    def prepare(j, carry):
        part = own[:, pl.ds(pl.multiple_of(j * 4 * box, 4 * box), 4 * box)]
        res = jnp.dot(part, place_own, preferred_element_type=jnp.float32)
        for i in range(4):
            start = pl.multiple_of((4 * j + i) * box, box)
            phi[pl.ds(start, box), :] = res[:, 2 * box * i : 2 * box * (i + 1)]
            wx = column[pl.ds(4 * j + i, 1), :]
            sq = column[...] + lane_sq[0:1, :] + wx + (8.0 * math.pi / box) ** 2
            green[pl.ds(start, box), :] = 1.0 / sq
        return carry

    lax.fori_loop(0, chunks, prepare, 0)

    def one_pair(p, carry):
        unit_a, unit_b = 2 * p, 2 * p + 1

        place = jnp.concatenate(
            [placing(box, 0, moves[unit_a, 2]), placing(box, 1, moves[unit_b, 2])], axis=0
        )
        for q in range(PAIRS):

            @pl.when(p == q)
            def _():
                cells = ORDER[2 * q : 2 * q + 2]
                blocks, rows = [], []
                for which, (i, j) in enumerate(cells):
                    row = CELLS.index((i, j))
                    if (i, j) == (0, 0):
                        blocks.append(own)
                        rows.append(tally[row : row + 1, :] * (2.0 if which == 0 else 0.0))
                        continue
                    slot = SLOTS.index((i, j))
                    for copy in arrive[i, j]:
                        copy.wait_recv()
                    blocks.append(landed.at[slot])
                    back_row = CELLS.index((-i, -j))
                    rows.append(
                        tally[row : row + 1, :] + landed_tally[slot, back_row : back_row + 1, :]
                    )
                if q == 1:
                    for pair in relay:
                        for copy in pair:
                            copy.start()
                weights[...] = jnp.where(low_half[0:8], rows[0], rows[1])

                def stage(j, inner):
                    here = pl.ds(pl.multiple_of(j * 4 * box, 4 * box), 4 * box)
                    part = jnp.concatenate([block[:, here] for block in blocks], axis=1)
                    res = jnp.dot(part, place, preferred_element_type=jnp.float32)
                    for i in range(4):
                        start = pl.multiple_of((4 * j + i) * 2 * box + box // 2, box // 2)
                        staged[pl.ds(start, box), :] = res[:, 2 * box * i : 2 * box * (i + 1)]
                    return inner

                lax.fori_loop(0, chunks, stage, 0)

        def fetch(y, unit):
            source = y + moves[unit, 1]
            inside = (source >= 0) & (source < box)
            row = jnp.clip(source, 0, box - 1) * 2 * box + box // 2 + moves[unit, 0]
            return staged[pl.ds(row, box), :] * jnp.where(inside, 1.0, 0.0)

        def forward(g, inner):
            tiles = []
            for i in range(GROUP):
                y = g * GROUP + i
                start = pl.multiple_of(y * box, box)
                moved = jnp.where(low_half, fetch(y, unit_a), fetch(y, unit_b))
                partner[pl.ds(start, box), :] = moved
                tiles.append(moved * phi[pl.ds(start, box), :])
            tiles = apply_right(right_f[...], apply_left(left_f[...], tiles))
            for i in range(GROUP):
                start = pl.multiple_of((g * GROUP + i) * pitch, 8)
                work[pl.ds(start, box), :] = tiles[i]
            return inner

        lax.fori_loop(0, box // GROUP, forward, 0)

        def middle(g, inner):
            tiles = []
            for i in range(GROUP):
                tiles.append(work[pl.ds(g * GROUP + i, box, stride=pitch), :])
            tiles = apply_left(left_f[...], tiles)
            for i in range(GROUP):
                start = pl.multiple_of((g * GROUP + i) * box, box)
                tiles[i] = tiles[i] * green[pl.ds(start, box), :]
            tiles = apply_left(left_i[...], tiles)
            for i in range(GROUP):
                work[pl.ds(g * GROUP + i, box, stride=pitch), :] = tiles[i]
            return inner

        lax.fori_loop(0, box // GROUP, middle, 0)

        def back(g, inner):
            tiles = []
            for i in range(GROUP):
                start = pl.multiple_of((g * GROUP + i) * pitch, 8)
                tiles.append(work[pl.ds(start, box), :])
            tiles = apply_left(left_i[...], apply_right(right_i[...], tiles))
            weight = weights[0:1, :]
            for i in range(GROUP):
                start = pl.multiple_of((g * GROUP + i) * box, box)
                here = pl.ds(start, box)
                total[here, :] = total[here, :] + tiles[i] * partner[here, :] * weight
            return inner

        lax.fori_loop(0, box // GROUP, back, 0)
        return carry

    lax.fori_loop(0, PAIRS, one_pair, 0)

    def finish(j, carry):
        even = total[pl.ds(pl.multiple_of(2 * j * box, box), box), :]
        odd = total[pl.ds(pl.multiple_of((2 * j + 1) * box, box), box), :]
        even = even + pltpu.roll(even, box, 1)
        odd = odd + pltpu.roll(odd, box, 1)
        here = pl.ds(pl.multiple_of(j * 2 * box, 2 * box), 2 * box)
        out[:, here] = jnp.where(low_half, even, odd)
        return carry

    lax.fori_loop(0, box // 2, finish, 0)
    for pair in first + relay:
        for copy in pair:
            copy.wait_send()


def body(orbitals, offsets, pair_list, pair_mask):
    box, flat = orbitals.shape[1:]
    consts = tuple(jnp.asarray(t) for t in tables(box))
    vmem = pl.BlockSpec(memory_space=pltpu.VMEM)
    smem = pl.BlockSpec(memory_space=pltpu.SMEM)
    rows = box * box
    macs = PAIRS * 7 * 4096 * 65536
    slots = len(SLOTS)
    out = pl.pallas_call(
        functools.partial(kernel, lax.axis_size("dx"), lax.axis_size("dy"), box),
        out_shape=jax.ShapeDtypeStruct((box, flat), jnp.float32),
        in_specs=[smem] * 3 + [vmem] * (len(consts) + 1),
        out_specs=vmem,
        scratch_shapes=[
            pltpu.VMEM((2 * rows, 2 * box), jnp.float32),
            pltpu.VMEM((rows, 2 * box), jnp.float32),
            pltpu.VMEM((box * (box + 8), 2 * box), jnp.float32),
            pltpu.VMEM((rows, 2 * box), jnp.float32),
            pltpu.VMEM((rows, 2 * box), jnp.float32),
            pltpu.VMEM((rows, 2 * box), jnp.float32),
            pltpu.VMEM((16, 2 * box), jnp.float32),
            pltpu.VMEM((8, 2 * box), jnp.float32),
            pltpu.SMEM((len(ORDER), 3), jnp.int32),
            pltpu.VMEM((slots, box, flat), jnp.bfloat16),
            pltpu.VMEM((slots, 16, 2 * box), jnp.float32),
        ]
        + [pltpu.SemaphoreType.DMA((slots,))] * 4,
        compiler_params=pltpu.CompilerParams(
            vmem_limit_bytes=48 * 1024 * 1024, collective_id=0, has_side_effects=True
        ),
        cost_estimate=pl.CostEstimate(
            flops=2 * macs, bytes_accessed=10 * rows * box * 2, transcendentals=0
        ),
    )(offsets, pair_list, pair_mask, *consts, orbitals[0])
    return out[None]


def solution(mesh):
    placed = (P(("dx", "dy"), None, None), P(), P(("dx", "dy"), None), P(("dx", "dy")))
    return jax.shard_map(
        body, mesh=mesh, in_specs=placed, out_specs=P(("dx", "dy"), None, None), check_vma=False
    )
```

time: 163 us -> 95.5 us (0.59)
  the two profiles are of different devices: /device:TPU:7 before, /device:TPU:1 now
where the time goes in v2:
time: 95.5 us; the launch traced here: 93.7 us
  Pallas kernels  85.5 us (90%)
  local copies, waits for them, and re-layouts  8.15 us (9%)
    pallas_call x1, Pallas kernels, body(): pl.pallas_call(functools.partial(kernel, lax.axis_size('dx'), lax.axis_si...  85.5 us
    unnamed x23, local copies, waits for them, and re-layouts  8.15 us

profile of v2, /device:TPU:1, one launch (start us, length us, event | category | flops | bytes accessed | tf_op | source)
XLA Modules:
  0.0 93.7 jit_solution(14677007853229790984)
XLA Ops:
  0.0 0.0 copy-start.9
  0.0 0.7 copy-done.9
  0.7 0.0 copy-start.8
  0.7 0.1 copy.12.refs_1_
  0.8 0.6 copy-done.8
  1.4 0.0 copy-start.1
  1.4 0.0 copy-start.7
  1.4 0.1 copy.11.refs_0_
  1.5 0.6 copy-done.1
  2.0 0.0 copy-done.7
  2.1 0.0 copy-start
  2.1 1.0 %copy-done = bf16[1,64,4096]{2,1,0:T(8,128)(2,1)S(1)} copy-done((bf16[1,64,4096]{2,1,0:T(8,128)(2,1)S(1)}, bf16[1,64,4096]{2,1,0:T(8,128)(2,1)}, u32[]{:S(2)}) %copy-start) | copy-done | bytes 524312
  3.1 0.0 copy-start.2
  3.1 0.9 copy-done.2
  4.0 0.0 copy-start.3
  4.0 0.9 copy-done.3
  4.9 0.0 copy-start.4
  4.9 0.8 copy-done.4
  5.7 0.0 copy-start.5
  5.7 0.8 copy-done.5
  6.4 0.0 copy-start.6
  6.4 0.8 copy-done.6
  7.2 85.5 %shard_map.100 = f32[64,4096]{1,0:T(8,128)S(1)} custom-call(s32[32,3]{1,0:T(8,128)S(1)} %copy.11.refs_0_, s32[8,2]{1,0:T(8,128)S(1)} %copy.12.refs_1_, s32[8]{0:T(128)S(1)} %copy-done.1, bf16[128,128]{1,0:T(8,128)(2,1)S(1)} %copy-done.6, bf16[128,128]{1,0:T(8,128)(2,1)S(1)} %copy-done.5, bf16[256,256]{1,0:T(8,128)(2,1)S(1)} %copy-done.3, ...), custom_call_target="tpu_custom_call" | custom-call | flops 18790481920 | bytes 5242880 | tf_op jit(solution)/shard_map/pallas_call | solution.py:311
  92.7 1.0 %copy.14 = f32[1,64,4096]{2,1,0:T(8,128)} copy(f32[1,64,4096]{2,1,0:T(8,128)S(1)} %bitcast.2) | data formatting | bytes 2097152
Async XLA Ops:
  0.0 0.7 copy-start.9
  0.7 0.7 copy-start.8
  1.4 0.7 copy-start.1
  1.4 0.7 copy-start.7
  2.1 1.0 %copy-start = (bf16[1,64,4096]{2,1,0:T(8,128)(2,1)S(1)}, bf16[1,64,4096]{2,1,0:T(8,128)(2,1)}, u32[]{:S(2)}) copy-start(bf16[1,64,4096]{2,1,0:T(8,128)(2,1)} %param.10) | copy-start | bytes 1572868
  3.1 0.9 copy-start.2
  4.0 0.9 copy-start.3
  4.9 0.8 copy-start.4
  5.7 0.8 copy-start.5
  6.4 0.8 copy-start.6

commit v3 on v2

--- a/solution.py
+++ b/solution.py
@@ -10,7 +10,9 @@
 from jax.experimental.pallas import tpu as pltpu
 from jax.sharding import PartitionSpec as P
 
-GROUP = 8
+GROUP = 16
+LEFT = 2
+RIGHT = 8
 CELLS = [(i, j) for i in (-1, 0, 1) for j in (-1, 0, 1)]
 SLOTS = [cell for cell in CELLS if cell != (0, 0)]
 ORDER = [(0, 0), (0, 0), (-1, 0), (1, 0), (0, -1), (0, 1), (-1, -1), (-1, 1), (1, -1), (1, 1)]
@@ -45,18 +47,8 @@
 
 def tables(box):
     rows, freq = basis(box)
-    wave = 2.0 * np.pi / box * freq
-    square = (wave * wave).astype(np.float32)
-    column = square[:, None] + np.zeros((1, 2 * box), np.float32)
-    lane = np.concatenate([square, square])[None, :] + np.zeros((8, 1), np.float32)
-    return (
-        left_table(rows),
-        left_table(rows.T),
-        right_table(rows.T),
-        right_table(rows),
-        column,
-        lane,
-    )
+    lefts = np.concatenate([left_table(rows), left_table(rows.T)], axis=1)
+    return np.concatenate([lefts, right_table(rows.T), right_table(rows)], axis=0)
 
 
 def split(value):
@@ -66,21 +58,27 @@
 
 
 def apply_left(table, tiles):
-    box = tiles[0].shape[0]
-    high, low = split(jnp.concatenate(tiles, axis=1))
-    both = jnp.concatenate([high, low], axis=0)
-    out = jnp.dot(table, both, preferred_element_type=jnp.float32)
-    out = out[:box] + out[box:]
-    return [out[:, 128 * i : 128 * (i + 1)] for i in range(len(tiles))]
+    box, lanes = tiles[0].shape
+    made = []
+    for first in range(0, len(tiles), LEFT):
+        high, low = split(jnp.concatenate(tiles[first : first + LEFT], axis=1))
+        both = jnp.concatenate([high, low], axis=0)
+        out = jnp.dot(table, both, preferred_element_type=jnp.float32)
+        out = out[:box] + out[box:]
+        made += [out[:, lanes * i : lanes * (i + 1)] for i in range(LEFT)]
+    return made
 
 
 def apply_right(table, tiles):
     box, lanes = tiles[0].shape
-    high, low = split(jnp.concatenate(tiles, axis=0))
-    both = jnp.concatenate([high, low], axis=1)
-    out = jnp.dot(both, table, preferred_element_type=jnp.float32)
-    out = out[:, :lanes] + out[:, lanes:]
-    return [out[box * i : box * (i + 1)] for i in range(len(tiles))]
+    made = []
+    for first in range(0, len(tiles), RIGHT):
+        high, low = split(jnp.concatenate(tiles[first : first + RIGHT], axis=0))
+        both = jnp.concatenate([high, low], axis=1)
+        out = jnp.dot(both, table, preferred_element_type=jnp.float32)
+        out = out[:, :lanes] + out[:, lanes:]
+        made += [out[box * i : box * (i + 1)] for i in range(RIGHT)]
+    return made
 
 
 def placing(box, which, move_z):
@@ -93,10 +91,11 @@
 
 
 def kernel(count_x, count_y, box, *refs):
-    offsets, pair_list, pair_mask, left_f, left_i, right_f, right_i, column, lane_sq, own = refs[:10]
-    out, staged, partner, work, total, phi, green = refs[10:17]
-    tally, weights, moves, landed, landed_tally = refs[17:22]
-    send_sem, recv_sem, tally_send, tally_recv = refs[22:]
+    offsets_in, list_in, mask_in, table_in, own_in = refs[:5]
+    out, staged, partner, work, total, phi, green = refs[5:12]
+    tally, weights, moves, landed, landed_tally = refs[12:17]
+    offsets, pair_list, pair_mask, table, own = refs[17:22]
+    send_sem, recv_sem, tally_send, tally_recv, local_sem = refs[22:]
     chunks = box // 4
     pitch = box + 8
 
@@ -120,11 +119,27 @@
             barrier, inc=1, device_id=target(*step), device_id_type=pl.DeviceIdType.MESH
         )
 
+    local = [
+        pltpu.make_async_copy(src, dst, local_sem.at[k])
+        for k, (src, dst) in enumerate(
+            (
+                (offsets_in, offsets),
+                (list_in, pair_list),
+                (mask_in, pair_mask),
+                (own_in, own),
+                (table_in, table),
+            )
+        )
+    ]
+    for copy in local:
+        copy.start()
     tally[...] = jnp.zeros_like(tally)
+    for copy in local[:3]:
+        copy.wait()
     for row, (i, j) in enumerate(CELLS):
         number = jnp.int32(0)
         for slot in range(pair_mask.shape[0]):
-            same = pair_list[slot, 1] == owner(i, j)
+            same = pair_list[1, slot] == owner(i, j)
             number = number + jnp.where(same, pair_mask[slot], 0)
         tally[row : row + 1, :] = jnp.full((1, 2 * box), 1.0, jnp.float32) * number.astype(
             jnp.float32
@@ -132,20 +147,20 @@
     mine = owner(0, 0)
     for unit, cell in enumerate(ORDER):
         for axis in range(3):
-            moves[unit, axis] = offsets[mine, axis] - offsets[owner(*cell), axis]
+            moves[unit, axis] = offsets[axis, mine] - offsets[axis, owner(*cell)]
 
     pl.semaphore_wait(barrier, 4)
 
     def copies(source, i, j):
         slot = SLOTS.index((source[0] - i, source[1] - j))
-        block, number = (own, tally)
+        block, number = (own_in, tally)
         if source != (0, 0):
             block = landed.at[SLOTS.index(source)]
             number = landed_tally.at[SLOTS.index(source)]
         made = []
         for src, dst, send, recv in (
+            (block, landed, send_sem, recv_sem),
             (number, landed_tally, tally_send, tally_recv),
-            (block, landed, send_sem, recv_sem),
         ):
             made.append(
                 pltpu.make_async_remote_copy(
@@ -174,18 +189,29 @@
     total[...] = jnp.zeros_like(total)
     place_own = placing(box, None, 0)
 
+    def square(index):
+        freq = jnp.where(index <= box // 2, index, index - box // 2).astype(jnp.float32)
+        return (2.0 * math.pi / box * freq) * (2.0 * math.pi / box * freq)
+
+    plane = square(lax.broadcasted_iota(jnp.int32, (box, 2 * box), 0))
+    plane = plane + square(jnp.where(low_half, lane, lane - box)) + (8.0 * math.pi / box) ** 2
+    local[3].wait()
+
     def prepare(j, carry):
         part = own[:, pl.ds(pl.multiple_of(j * 4 * box, 4 * box), 4 * box)]
         res = jnp.dot(part, place_own, preferred_element_type=jnp.float32)
         for i in range(4):
             start = pl.multiple_of((4 * j + i) * box, box)
             phi[pl.ds(start, box), :] = res[:, 2 * box * i : 2 * box * (i + 1)]
-            wx = column[pl.ds(4 * j + i, 1), :]
-            sq = column[...] + lane_sq[0:1, :] + wx + (8.0 * math.pi / box) ** 2
-            green[pl.ds(start, box), :] = 1.0 / sq
+            green[pl.ds(start, box), :] = 1.0 / (plane + square(4 * j + i))
         return carry
 
     lax.fori_loop(0, chunks, prepare, 0)
+    local[4].wait()
+    left_f = table.at[0 : 2 * box, 0 : 2 * box]
+    left_i = table.at[0 : 2 * box, 2 * box : 4 * box]
+    right_f = table.at[2 * box : 6 * box, :]
+    right_i = table.at[6 * box : 10 * box, :]
 
     def one_pair(p, carry):
         unit_a, unit_b = 2 * p, 2 * p + 1
@@ -302,16 +328,16 @@
 
 def body(orbitals, offsets, pair_list, pair_mask):
     box, flat = orbitals.shape[1:]
-    consts = tuple(jnp.asarray(t) for t in tables(box))
+    table = jnp.asarray(tables(box))
     vmem = pl.BlockSpec(memory_space=pltpu.VMEM)
-    smem = pl.BlockSpec(memory_space=pltpu.SMEM)
+    stay = pl.BlockSpec(memory_space=pl.ANY)
     rows = box * box
     macs = PAIRS * 7 * 4096 * 65536
     slots = len(SLOTS)
     out = pl.pallas_call(
         functools.partial(kernel, lax.axis_size("dx"), lax.axis_size("dy"), box),
         out_shape=jax.ShapeDtypeStruct((box, flat), jnp.float32),
-        in_specs=[smem] * 3 + [vmem] * (len(consts) + 1),
+        in_specs=[stay] * 5,
         out_specs=vmem,
         scratch_shapes=[
             pltpu.VMEM((2 * rows, 2 * box), jnp.float32),
@@ -325,15 +351,21 @@
             pltpu.SMEM((len(ORDER), 3), jnp.int32),
             pltpu.VMEM((slots, box, flat), jnp.bfloat16),
             pltpu.VMEM((slots, 16, 2 * box), jnp.float32),
+            pltpu.SMEM(offsets.shape[::-1], jnp.int32),
+            pltpu.SMEM(pair_list.shape[::-1], jnp.int32),
+            pltpu.SMEM(pair_mask.shape, jnp.int32),
+            pltpu.VMEM(table.shape, jnp.bfloat16),
+            pltpu.VMEM((box, flat), jnp.bfloat16),
         ]
-        + [pltpu.SemaphoreType.DMA((slots,))] * 4,
+        + [pltpu.SemaphoreType.DMA((slots,))] * 4
+        + [pltpu.SemaphoreType.DMA((5,))],
         compiler_params=pltpu.CompilerParams(
-            vmem_limit_bytes=48 * 1024 * 1024, collective_id=0, has_side_effects=True
+            vmem_limit_bytes=60 * 1024 * 1024, collective_id=0, has_side_effects=True
         ),
         cost_estimate=pl.CostEstimate(
             flops=2 * macs, bytes_accessed=10 * rows * box * 2, transcendentals=0
         ),
-    )(offsets, pair_list, pair_mask, *consts, orbitals[0])
+    )(offsets.T, pair_list.T, pair_mask, table, orbitals[0])
     return out[None]
 
 

time: 95.5 us -> 73.5 us (0.77)
  the two profiles are of different devices: /device:TPU:1 before, /device:TPU:0 now
where the time goes in v3:
time: 73.5 us; the launch traced here: 73.3 us
  Pallas kernels  71.1 us (97%)
  local copies, waits for them, and re-layouts  2.27 us (3%)
    pallas_call x1, Pallas kernels, body(): pl.pallas_call(functools.partial(kernel, lax.axis_size('dx'), lax.axis_si...  71.1 us
    unnamed x1, local copies, waits for them, and re-layouts  2.27 us

profile of v3, /device:TPU:0, one launch (start us, length us, event | category | flops | bytes accessed | tf_op | source)
XLA Modules:
  0.0 73.3 jit_solution(17950165601269545983)
XLA Ops:
  0.0 71.1 %shard_map.55 = f32[64,4096]{1,0:T(8,128)} custom-call(s32[3,32]{1,0:T(4,128)} %bitcast.6, s32[2,8]{1,0:T(2,128)} %bitcast.7, s32[8]{0:T(128)} %refs_2_.1, bf16[640,256]{1,0:T(8,128)(2,1)} %constant.2.clone.refs_3_, bf16[64,4096]{1,0:T(8,128)(2,1)} %bitcast.5), custom_call_target="tpu_custom_call" | custom-call | flops 18790481920 | bytes 5242880 | tf_op jit(solution)/shard_map/pallas_call | solution.py:337
  71.1 2.3 %copy.7 = f32[1,64,4096]{2,1,0:T(8,128)} copy(f32[1,64,4096]{2,1,0:T(8,128)} %bitcast.4) | data formatting | bytes 2097152

commit v4 on v3

--- a/solution.py
+++ b/solution.py
@@ -13,9 +13,10 @@
 GROUP = 16
 LEFT = 2
 RIGHT = 8
+CHUNKS = 8
 CELLS = [(i, j) for i in (-1, 0, 1) for j in (-1, 0, 1)]
 SLOTS = [cell for cell in CELLS if cell != (0, 0)]
-ORDER = [(0, 0), (0, 0), (-1, 0), (1, 0), (0, -1), (0, 1), (-1, -1), (-1, 1), (1, -1), (1, 1)]
+ORDER = [(0, 0), (0, 0), (0, -1), (0, 1), (-1, 0), (1, 0), (-1, -1), (-1, 1), (1, -1), (1, 1)]
 PAIRS = len(ORDER) // 2
 
 
@@ -197,16 +198,27 @@
     plane = plane + square(jnp.where(low_half, lane, lane - box)) + (8.0 * math.pi / box) ** 2
     local[3].wait()
 
+    def placed(j, blocks, table, write):
+        parts = []
+        for c in range(CHUNKS):
+            here = pl.ds(pl.multiple_of((j * CHUNKS + c) * 4 * box, 4 * box), 4 * box)
+            parts.append(jnp.concatenate([block[:, here] for block in blocks], axis=1))
+        res = jnp.dot(jnp.concatenate(parts, axis=0), table, preferred_element_type=jnp.float32)
+        for c in range(CHUNKS):
+            for i in range(4):
+                y = (j * CHUNKS + c) * 4 + i
+                write(y, res[box * c : box * (c + 1), 2 * box * i : 2 * box * (i + 1)])
+
     def prepare(j, carry):
-        part = own[:, pl.ds(pl.multiple_of(j * 4 * box, 4 * box), 4 * box)]
-        res = jnp.dot(part, place_own, preferred_element_type=jnp.float32)
-        for i in range(4):
-            start = pl.multiple_of((4 * j + i) * box, box)
-            phi[pl.ds(start, box), :] = res[:, 2 * box * i : 2 * box * (i + 1)]
-            green[pl.ds(start, box), :] = 1.0 / (plane + square(4 * j + i))
+        def write(y, tile):
+            start = pl.multiple_of(y * box, box)
+            phi[pl.ds(start, box), :] = tile
+            green[pl.ds(start, box), :] = 1.0 / (plane + square(y))
+
+        placed(j, [own], place_own, write)
         return carry
 
-    lax.fori_loop(0, chunks, prepare, 0)
+    lax.fori_loop(0, chunks // CHUNKS, prepare, 0)
     local[4].wait()
     left_f = table.at[0 : 2 * box, 0 : 2 * box]
     left_i = table.at[0 : 2 * box, 2 * box : 4 * box]
@@ -232,29 +244,25 @@
                         rows.append(tally[row : row + 1, :] * (2.0 if which == 0 else 0.0))
                         continue
                     slot = SLOTS.index((i, j))
-                    for copy in arrive[i, j]:
-                        copy.wait_recv()
+                    if j != 0:
+                        for copy in arrive[i, j]:
+                            copy.wait_recv()
                     blocks.append(landed.at[slot])
                     back_row = CELLS.index((-i, -j))
                     rows.append(
                         tally[row : row + 1, :] + landed_tally[slot, back_row : back_row + 1, :]
                     )
-                if q == 1:
-                    for pair in relay:
-                        for copy in pair:
-                            copy.start()
                 weights[...] = jnp.where(low_half[0:8], rows[0], rows[1])
 
                 def stage(j, inner):
-                    here = pl.ds(pl.multiple_of(j * 4 * box, 4 * box), 4 * box)
-                    part = jnp.concatenate([block[:, here] for block in blocks], axis=1)
-                    res = jnp.dot(part, place, preferred_element_type=jnp.float32)
-                    for i in range(4):
-                        start = pl.multiple_of((4 * j + i) * 2 * box + box // 2, box // 2)
-                        staged[pl.ds(start, box), :] = res[:, 2 * box * i : 2 * box * (i + 1)]
+                    def write(y, tile):
+                        start = pl.multiple_of(y * 2 * box + box // 2, box // 2)
+                        staged[pl.ds(start, box), :] = tile
+
+                    placed(j, blocks, place, write)
                     return inner
 
-                lax.fori_loop(0, chunks, stage, 0)
+                lax.fori_loop(0, chunks // CHUNKS, stage, 0)
 
         def fetch(y, unit):
             source = y + moves[unit, 1]
@@ -277,6 +285,15 @@
             return inner
 
         lax.fori_loop(0, box // GROUP, forward, 0)
+
+        @pl.when(p == 1)
+        def _():
+            for k, i in enumerate((-1, 1)):
+                for copy in arrive[i, 0]:
+                    copy.wait_recv()
+                for pair in relay[2 * k : 2 * k + 2]:
+                    for copy in pair:
+                        copy.start()
 
         def middle(g, inner):
             tiles = []

time: 73.5 us -> 60.6 us (0.82)
  Pallas kernels: 71.1 us -> 58.2 us
    pallas_call x1, Pallas kernels: 71.1 us -> 58.2 us  [body(): pl.pallas_call(functools.partial(kernel, lax.axis_size('dx'), lax.axis_si...]
where the time goes in v4:
time: 60.6 us; the launch traced here: 60.4 us
  Pallas kernels  58.2 us (96%)
  local copies, waits for them, and re-layouts  2.27 us (4%)
    pallas_call x1, Pallas kernels, body(): pl.pallas_call(functools.partial(kernel, lax.axis_size('dx'), lax.axis_si...  58.2 us
    unnamed x1, local copies, waits for them, and re-layouts  2.27 us

profile of v4, /device:TPU:0, one launch (start us, length us, event | category | flops | bytes accessed | tf_op | source)
XLA Modules:
  0.0 60.4 jit_solution(6227027179731786611)
XLA Ops:
  0.0 58.2 %shard_map.55 = f32[64,4096]{1,0:T(8,128)} custom-call(s32[3,32]{1,0:T(4,128)} %bitcast.6, s32[2,8]{1,0:T(2,128)} %bitcast.7, s32[8]{0:T(128)} %refs_2_.1, bf16[640,256]{1,0:T(8,128)(2,1)} %constant.2.clone.refs_3_, bf16[64,4096]{1,0:T(8,128)(2,1)} %bitcast.5), custom_call_target="tpu_custom_call" | custom-call | flops 18790481920 | bytes 5242880 | tf_op jit(solution)/shard_map/pallas_call | solution.py:354
  58.2 2.3 %copy.7 = f32[1,64,4096]{2,1,0:T(8,128)} copy(f32[1,64,4096]{2,1,0:T(8,128)} %bitcast.4) | data formatting | bytes 2097152

commit v5 on v4

--- a/solution.py
+++ b/solution.py
@@ -15,9 +15,7 @@
 RIGHT = 8
 CHUNKS = 8
 CELLS = [(i, j) for i in (-1, 0, 1) for j in (-1, 0, 1)]
-SLOTS = [cell for cell in CELLS if cell != (0, 0)]
-ORDER = [(0, 0), (0, 0), (0, -1), (0, 1), (-1, 0), (1, 0), (-1, -1), (-1, 1), (1, -1), (1, 1)]
-PAIRS = len(ORDER) // 2
+PAIRS = 5
 
 
 def basis(box):
@@ -110,12 +108,31 @@
         x, y = domain(i, j)
         return x * count_y + y
 
-    def target(i, j):
+    def slot_of(i, j):
+        return 3 * (i + 1) + j + 1
+
+    edge = (place_x == 0) | (place_x == count_x - 1)
+    near = jnp.where(place_x == 0, 1, -1)
+    side = 1 - 2 * lax.rem(place_y, 2)
+    order = [
+        (0, 0),
+        (0, side),
+        (0, -side),
+        (near, 0),
+        (near, side),
+        None,
+        (near, -side),
+        (-near, 0),
+        (-near, side),
+        (-near, -side),
+    ]
+
+    def target(i, j, along):
         x, y = domain(i, j)
-        return {"dx": x} if j == 0 else {"dy": y}
+        return {"dx": x} if along == "dx" else {"dy": y}
 
     barrier = pltpu.get_barrier_semaphore()
-    for step in ((1, 0), (-1, 0), (0, 1), (0, -1)):
+    for step in ((1, 0, "dx"), (-1, 0, "dx"), (0, 1, "dy"), (0, -1, "dy")):
         pl.semaphore_signal(
             barrier, inc=1, device_id=target(*step), device_id_type=pl.DeviceIdType.MESH
         )
@@ -146,42 +163,66 @@
             jnp.float32
         )
     mine = owner(0, 0)
-    for unit, cell in enumerate(ORDER):
+    for unit, cell in enumerate(order):
+        other = mine if cell is None else owner(*cell)
         for axis in range(3):
-            moves[unit, axis] = offsets[axis, mine] - offsets[axis, owner(*cell)]
+            moves[unit, axis] = offsets[axis, mine] - offsets[axis, other]
 
     pl.semaphore_wait(barrier, 4)
 
-    def copies(source, i, j):
-        slot = SLOTS.index((source[0] - i, source[1] - j))
+    def copies(source, i, j, along, relayed=False):
+        slot = slot_of(source[0] - i, source[1] - j)
         block, number = (own_in, tally)
-        if source != (0, 0):
-            block = landed.at[SLOTS.index(source)]
-            number = landed_tally.at[SLOTS.index(source)]
-        made = []
+        if relayed:
+            block = landed.at[slot_of(*source)]
+            number = landed_tally.at[slot_of(*source)]
+        return [
+            pltpu.make_async_remote_copy(
+                src_ref=src,
+                dst_ref=dst.at[slot],
+                send_sem=send.at[slot],
+                recv_sem=recv.at[slot],
+                device_id=target(i, j, along),
+                device_id_type=pl.DeviceIdType.MESH,
+            )
+            for src, dst, send, recv in (
+                (block, landed, send_sem, recv_sem),
+                (number, landed_tally, tally_send, tally_recv),
+            )
+        ]
+
+    def start(made):
+        for copy in made:
+            copy.start()
+
+    def arrived(i, j):
+        slot = slot_of(i, j)
         for src, dst, send, recv in (
-            (block, landed, send_sem, recv_sem),
-            (number, landed_tally, tally_send, tally_recv),
+            (own_in, landed, send_sem, recv_sem),
+            (tally, landed_tally, tally_send, tally_recv),
         ):
-            made.append(
-                pltpu.make_async_remote_copy(
-                    src_ref=src,
-                    dst_ref=dst.at[slot],
-                    send_sem=send.at[slot],
-                    recv_sem=recv.at[slot],
-                    device_id=target(i, j),
-                    device_id_type=pl.DeviceIdType.MESH,
-                )
-            )
-        return made
-
-    first = [copies((0, 0), *step) for step in ((1, 0), (-1, 0), (0, 1), (0, -1))]
-    relay = [copies((i, 0), 0, j) for i in (-1, 1) for j in (1, -1)]
-    arrive = {(-1, 0): first[0], (1, 0): first[1], (0, -1): first[2], (0, 1): first[3]}
-    arrive.update({(-1, -1): relay[0], (-1, 1): relay[1], (1, -1): relay[2], (1, 1): relay[3]})
-    for pair in first:
-        for copy in pair:
-            copy.start()
+            pltpu.make_async_remote_copy(
+                src_ref=src,
+                dst_ref=dst.at[slot],
+                send_sem=send.at[slot],
+                recv_sem=recv.at[slot],
+                device_id=target(0, 1, "dy"),
+                device_id_type=pl.DeviceIdType.MESH,
+            ).wait_recv()
+
+    own_y = [copies((0, 0), 0, j, "dy") for j in (-side, side)]
+    to_near = copies((0, 0), near, 0, "dx")
+    to_far = copies((0, 0), -near, 0, "dx")
+    relay_near = [copies((near, 0), 0, j, "dy", True) for j in (-side, side)]
+    relay_far = [copies((-near, 0), 0, j, "dy", True) for j in (-side, side)]
+    start(to_near)
+
+    @pl.when(jnp.logical_not(edge))
+    def _():
+        start(to_far)
+
+    for made in own_y:
+        start(made)
 
     lane = lax.broadcasted_iota(jnp.int32, (box, 2 * box), 1)
     low_half = lane < box
@@ -211,9 +252,9 @@
 
     def prepare(j, carry):
         def write(y, tile):
-            start = pl.multiple_of(y * box, box)
-            phi[pl.ds(start, box), :] = tile
-            green[pl.ds(start, box), :] = 1.0 / (plane + square(y))
+            begin = pl.multiple_of(y * box, box)
+            phi[pl.ds(begin, box), :] = tile
+            green[pl.ds(begin, box), :] = 1.0 / (plane + square(y))
 
         placed(j, [own], place_own, write)
         return carry
@@ -235,22 +276,19 @@
 
             @pl.when(p == q)
             def _():
-                cells = ORDER[2 * q : 2 * q + 2]
                 blocks, rows = [], []
-                for which, (i, j) in enumerate(cells):
-                    row = CELLS.index((i, j))
-                    if (i, j) == (0, 0):
+                for unit in (2 * q, 2 * q + 1):
+                    if order[unit] is None or unit == 0:
+                        row = slot_of(0, 0)
                         blocks.append(own)
-                        rows.append(tally[row : row + 1, :] * (2.0 if which == 0 else 0.0))
+                        rows.append(tally[row : row + 1, :] * (2.0 if unit == 0 else 0.0))
                         continue
-                    slot = SLOTS.index((i, j))
-                    if j != 0:
-                        for copy in arrive[i, j]:
-                            copy.wait_recv()
+                    if unit not in (3, 7):
+                        arrived(*order[unit])
+                    slot = slot_of(*order[unit])
                     blocks.append(landed.at[slot])
-                    back_row = CELLS.index((-i, -j))
                     rows.append(
-                        tally[row : row + 1, :] + landed_tally[slot, back_row : back_row + 1, :]
+                        tally[pl.ds(slot, 1), :] + landed_tally[slot, pl.ds(8 - slot, 1), :]
                     )
                 weights[...] = jnp.where(low_half[0:8], rows[0], rows[1])
 
@@ -286,14 +324,15 @@
 
         lax.fori_loop(0, box // GROUP, forward, 0)
 
-        @pl.when(p == 1)
+        @pl.when((p == 0) & edge)
         def _():
-            for k, i in enumerate((-1, 1)):
-                for copy in arrive[i, 0]:
-                    copy.wait_recv()
-                for pair in relay[2 * k : 2 * k + 2]:
-                    for copy in pair:
-                        copy.start()
+            start(to_far)
+
+        @pl.when(p == 2)
+        def _():
+            arrived(-near, 0)
+            for made in relay_far:
+                start(made)
 
         def middle(g, inner):
             tiles = []
@@ -324,6 +363,13 @@
             return inner
 
         lax.fori_loop(0, box // GROUP, back, 0)
+
+        @pl.when(p == 0)
+        def _():
+            arrived(near, 0)
+            for made in relay_near:
+                start(made)
+
         return carry
 
     lax.fori_loop(0, PAIRS, one_pair, 0)
@@ -338,8 +384,8 @@
         return carry
 
     lax.fori_loop(0, box // 2, finish, 0)
-    for pair in first + relay:
-        for copy in pair:
+    for made in [to_near, to_far] + own_y + relay_near + relay_far:
+        for copy in made:
             copy.wait_send()
 
 
@@ -350,7 +396,7 @@
     stay = pl.BlockSpec(memory_space=pl.ANY)
     rows = box * box
     macs = PAIRS * 7 * 4096 * 65536
-    slots = len(SLOTS)
+    slots = len(CELLS)
     out = pl.pallas_call(
         functools.partial(kernel, lax.axis_size("dx"), lax.axis_size("dy"), box),
         out_shape=jax.ShapeDtypeStruct((box, flat), jnp.float32),
@@ -365,7 +411,7 @@
             pltpu.VMEM((rows, 2 * box), jnp.float32),
             pltpu.VMEM((16, 2 * box), jnp.float32),
             pltpu.VMEM((8, 2 * box), jnp.float32),
-            pltpu.SMEM((len(ORDER), 3), jnp.int32),
+            pltpu.SMEM((2 * PAIRS, 3), jnp.int32),
             pltpu.VMEM((slots, box, flat), jnp.bfloat16),
             pltpu.VMEM((slots, 16, 2 * box), jnp.float32),
             pltpu.SMEM(offsets.shape[::-1], jnp.int32),

time: 60.6 us -> 57.3 us (0.946)
  the two profiles are of different devices: /device:TPU:0 before, /device:TPU:1 now
where the time goes in v5:
time: 57.3 us; the launch traced here: 57.2 us
  Pallas kernels  54.9 us (96%)
  local copies, waits for them, and re-layouts  2.27 us (4%)
    pallas_call x1, Pallas kernels, body(): pl.pallas_call(functools.partial(kernel, lax.axis_size('dx'), lax.axis_si...  54.9 us
    unnamed x1, local copies, waits for them, and re-layouts  2.27 us

profile of v5, /device:TPU:1, one launch (start us, length us, event | category | flops | bytes accessed | tf_op | source)
XLA Modules:
  0.0 57.2 jit_solution(11635976883080722213)
XLA Ops:
  0.0 54.9 %shard_map.55 = f32[64,4096]{1,0:T(8,128)} custom-call(s32[3,32]{1,0:T(4,128)} %bitcast.6, s32[2,8]{1,0:T(2,128)} %bitcast.7, s32[8]{0:T(128)} %refs_2_.1, bf16[640,256]{1,0:T(8,128)(2,1)} %constant.2.clone.refs_3_, bf16[64,4096]{1,0:T(8,128)(2,1)} %bitcast.5), custom_call_target="tpu_custom_call" | custom-call | flops 18790481920 | bytes 5242880 | tf_op jit(solution)/shard_map/pallas_call | solution.py:400
  54.9 2.3 %copy.7 = f32[1,64,4096]{2,1,0:T(8,128)} copy(f32[1,64,4096]{2,1,0:T(8,128)} %bitcast.4) | data formatting | bytes 2097152

commit v6 on v5

--- a/solution.py
+++ b/solution.py
@@ -36,7 +36,7 @@
 
 def left_table(matrix):
     high, low = split_np(matrix)
-    return np.block([[high, high], [low, np.zeros_like(low)]])
+    return np.concatenate([high, high, low, np.zeros_like(low)], axis=1)
 
 
 def right_table(matrix):
@@ -46,7 +46,7 @@
 
 def tables(box):
     rows, freq = basis(box)
-    lefts = np.concatenate([left_table(rows), left_table(rows.T)], axis=1)
+    lefts = np.concatenate([left_table(rows), left_table(rows.T)], axis=0)
     return np.concatenate([lefts, right_table(rows.T), right_table(rows)], axis=0)
 
 
@@ -61,9 +61,8 @@
     made = []
     for first in range(0, len(tiles), LEFT):
         high, low = split(jnp.concatenate(tiles[first : first + LEFT], axis=1))
-        both = jnp.concatenate([high, low], axis=0)
-        out = jnp.dot(table, both, preferred_element_type=jnp.float32)
-        out = out[:box] + out[box:]
+        terms = jnp.concatenate([high, low, high], axis=0)
+        out = jnp.dot(table, terms, preferred_element_type=jnp.float32)
         made += [out[:, lanes * i : lanes * (i + 1)] for i in range(LEFT)]
     return made
 
@@ -151,6 +150,8 @@
     ]
     for copy in local:
         copy.start()
+    staged[...] = jnp.zeros_like(staged)
+    total[...] = jnp.zeros_like(total)
     tally[...] = jnp.zeros_like(tally)
     for copy in local[:3]:
         copy.wait()
@@ -227,8 +228,6 @@
     lane = lax.broadcasted_iota(jnp.int32, (box, 2 * box), 1)
     low_half = lane < box
 
-    staged[...] = jnp.zeros_like(staged)
-    total[...] = jnp.zeros_like(total)
     place_own = placing(box, None, 0)
 
     def square(index):
@@ -261,8 +260,8 @@
 
     lax.fori_loop(0, chunks // CHUNKS, prepare, 0)
     local[4].wait()
-    left_f = table.at[0 : 2 * box, 0 : 2 * box]
-    left_i = table.at[0 : 2 * box, 2 * box : 4 * box]
+    left_f = table.at[0:box, 0 : 3 * box]
+    left_i = table.at[box : 2 * box, 0 : 3 * box]
     right_f = table.at[2 * box : 6 * box, :]
     right_i = table.at[6 * box : 10 * box, :]
 
@@ -305,8 +304,8 @@
         def fetch(y, unit):
             source = y + moves[unit, 1]
             inside = (source >= 0) & (source < box)
-            row = jnp.clip(source, 0, box - 1) * 2 * box + box // 2 + moves[unit, 0]
-            return staged[pl.ds(row, box), :] * jnp.where(inside, 1.0, 0.0)
+            row = jnp.where(inside, source, box) * 2 * box + box // 2 + moves[unit, 0]
+            return staged[pl.ds(row, box), :]
 
         def forward(g, inner):
             tiles = []
@@ -403,7 +402,7 @@
         in_specs=[stay] * 5,
         out_specs=vmem,
         scratch_shapes=[
-            pltpu.VMEM((2 * rows, 2 * box), jnp.float32),
+            pltpu.VMEM((2 * rows + 2 * box, 2 * box), jnp.float32),
             pltpu.VMEM((rows, 2 * box), jnp.float32),
             pltpu.VMEM((box * (box + 8), 2 * box), jnp.float32),
             pltpu.VMEM((rows, 2 * box), jnp.float32),

time: 57.3 us -> 57.2 us (level)
  no operation moved by 1% of the time
where the time goes in v6:
time: 57.2 us; the launch traced here: 57 us
  Pallas kernels  54.8 us (96%)
  local copies, waits for them, and re-layouts  2.27 us (4%)
    pallas_call x1, Pallas kernels, body(): pl.pallas_call(functools.partial(kernel, lax.axis_size('dx'), lax.axis_si...  54.8 us
    unnamed x1, local copies, waits for them, and re-layouts  2.27 us

profile of v6, /device:TPU:1, one launch (start us, length us, event | category | flops | bytes accessed | tf_op | source)
XLA Modules:
  0.0 57.0 jit_solution(9911722608211331437)
XLA Ops:
  0.0 54.8 %shard_map.55 = f32[64,4096]{1,0:T(8,128)} custom-call(s32[3,32]{1,0:T(4,128)} %bitcast.6, s32[2,8]{1,0:T(2,128)} %bitcast.7, s32[8]{0:T(128)} %refs_2_.1, bf16[640,256]{1,0:T(8,128)(2,1)} %constant.2.clone.refs_3_, bf16[64,4096]{1,0:T(8,128)(2,1)} %bitcast.5), custom_call_target="tpu_custom_call" | custom-call | flops 18790481920 | bytes 5242880 | tf_op jit(solution)/shard_map/pallas_call | solution.py:399
  54.8 2.3 %copy.7 = f32[1,64,4096]{2,1,0:T(8,128)} copy(f32[1,64,4096]{2,1,0:T(8,128)} %bitcast.4) | data formatting | bytes 2097152

commit v7 on v6

--- a/solution.py
+++ b/solution.py
@@ -259,6 +259,11 @@
         return carry
 
     lax.fori_loop(0, chunks // CHUNKS, prepare, 0)
+
+    @pl.when(edge)
+    def _():
+        start(to_far)
+
     local[4].wait()
     left_f = table.at[0:box, 0 : 3 * box]
     left_i = table.at[box : 2 * box, 0 : 3 * box]
@@ -322,10 +327,6 @@
             return inner
 
         lax.fori_loop(0, box // GROUP, forward, 0)
-
-        @pl.when((p == 0) & edge)
-        def _():
-            start(to_far)
 
         @pl.when(p == 2)
         def _():

time: 57.2 us -> 57.2 us (level)
  no operation moved by 1% of the time
where the time goes in v7:
time: 57.2 us; the launch traced here: 57 us
  Pallas kernels  54.8 us (96%)
  local copies, waits for them, and re-layouts  2.27 us (4%)
    pallas_call x1, Pallas kernels, body(): pl.pallas_call(functools.partial(kernel, lax.axis_size('dx'), lax.axis_si...  54.8 us
    unnamed x1, local copies, waits for them, and re-layouts  2.27 us

profile of v7, /device:TPU:1, one launch (start us, length us, event | category | flops | bytes accessed | tf_op | source)
XLA Modules:
  0.0 57.0 jit_solution(3901130725839387655)
XLA Ops:
  0.0 54.8 %shard_map.55 = f32[64,4096]{1,0:T(8,128)} custom-call(s32[3,32]{1,0:T(4,128)} %bitcast.6, s32[2,8]{1,0:T(2,128)} %bitcast.7, s32[8]{0:T(128)} %refs_2_.1, bf16[640,256]{1,0:T(8,128)(2,1)} %constant.2.clone.refs_3_, bf16[64,4096]{1,0:T(8,128)(2,1)} %bitcast.5), custom_call_target="tpu_custom_call" | custom-call | flops 18790481920 | bytes 5242880 | tf_op jit(solution)/shard_map/pallas_call | solution.py:400
  54.8 2.3 %copy.7 = f32[1,64,4096]{2,1,0:T(8,128)} copy(f32[1,64,4096]{2,1,0:T(8,128)} %bitcast.4) | data formatting | bytes 2097152
